TPU v7x, 128 devices: a whole 4x4x4 slice. The times are simulated.
128 devices in a mesh: row: 16 (over x, z_lo, core), col: 8 (over y, z_hi).
Axes of the slice: x: 4, y: 4, z: 4 (z_hi: 2, z_lo: 2; z = z_hi * 2 + z_lo), core: 2. Of those that a mesh axis runs over, the one named last changes fastest.
Arguments:
- pair_rep: bfloat16 [768, 768, 256], P('row', 'col'), may hold values from -6 to 6
- single_rep: bfloat16 [768, 768], replicated, may hold values from -6 to 6
- length: int32 [1], replicated, may hold values from 384 to 768
- pair_gain: float32 [256], replicated, may hold values from 0.25 to 1.75
- pair_proj: bfloat16 [4, 256, 256], replicated, may hold values from -0.375 to 0.375
- bias_weight: bfloat16 [256, 8], replicated, may hold values from -12 to 12
- pair_out_weight: bfloat16 [256, 256], replicated, may hold values from -1 to 1
- single_gain: float32 [768], replicated, may hold values from 0.25 to 1.75
- single_proj: bfloat16 [4, 768, 768], P(None, None, 'col'), may hold values from -0.21875 to 0.21875
- bias_norm_gain: float32 [256], replicated, may hold values from 0.25 to 1.75
- single_bias_weight: bfloat16 [256, 16], replicated, may hold values from -12 to 12
- single_out_weight: bfloat16 [768, 768], P('col'), may hold values from -0.625 to 0.625
Outputs:
- pair_out: bfloat16 [768, 768, 256], P('row', 'col')
- single_out: bfloat16 [768, 768], P('row', 'col')
Inputs may be any that keep to these rules, and one draw needn't show every extreme that they name: Positions from length[0] on are padding and never serve as keys.
All inputs are finite; a program needn't handle non-finite values.
Results may differ from a plain program's by a relative error of at most 0.019.
Values may be sent and summed in bfloat16 or wider, within the bound.
No kernel may reach another device: no remote copies, remote signals or barrier semaphores. Data moves between devices by JAX's collectives and lax.ppermute only.
A program may use at most 128 MiB of HBM per device.

v0:
```python
import math

import jax
import jax.numpy as jnp
from jax import lax
from jax.sharding import PartitionSpec as P

PAIR_HEADS = 8
PAIR_HEAD_DIM = 32
SINGLE_HEAD_DIM = 48


masked_value = -1e30


def normalize(values, scales):
    floated = values.astype(jnp.float32)
    center = jnp.mean(floated, axis=-1, keepdims=True)
    spread = jnp.mean(jnp.square(floated - center), axis=-1, keepdims=True)
    return ((floated - center) * lax.rsqrt(spread + 1e-05) * scales).astype(jnp.bfloat16)


def project(inputs, matrix):
    return jnp.dot(inputs, matrix, preferred_element_type=jnp.float32).astype(jnp.bfloat16)


def per_device(
    pair_rep,
    single_rep,
    length,
    pair_gain,
    pair_proj,
    bias_weight,
    pair_out_weight,
    single_gain,
    single_proj,
    bias_norm_gain,
    single_bias_weight,
    single_out_weight,
):
    rows_here, cols_here, channels = pair_rep.shape
    tokens = rows_here * lax.axis_size("row")
    valid_length = length[0]
    pair_scale = 1.0 / math.sqrt(PAIR_HEAD_DIM)
    normed = normalize(pair_rep, pair_gain)
    local_bias = jnp.einsum(
        "rcd,dh->hrc", normed, bias_weight, preferred_element_type=jnp.float32
    ).astype(jnp.bfloat16)
    row_band = lax.all_gather(local_bias, "col", axis=2, tiled=True)
    block_rows = math.gcd(rows_here, 4)
    groups = rows_here // block_rows
    queries = project(normed, pair_proj[0]).reshape(rows_here, cols_here, PAIR_HEADS, PAIR_HEAD_DIM)
    queries = jnp.transpose(queries, (0, 2, 1, 3))
    gating = jax.nn.sigmoid(jnp.dot(normed, pair_proj[3], preferred_element_type=jnp.float32))
    bias_full = lax.all_gather(row_band, "row", axis=1, tiled=True)
    tri_rows = lax.dynamic_slice_in_dim(bias_full, lax.axis_index("col") * cols_here, cols_here, 1)

    def regroup(tensor):
        return tensor.reshape((groups, block_rows) + tensor.shape[1:])

    running = jnp.full((rows_here, PAIR_HEADS, cols_here), masked_value, jnp.float32)
    totals = jnp.zeros((rows_here, PAIR_HEADS, cols_here), jnp.float32)
    summed = jnp.zeros((rows_here, PAIR_HEADS, cols_here, PAIR_HEAD_DIM), jnp.float32)
    pieces = (lax.all_gather(normed, "col", axis=1, tiled=True),)
    extent = pieces[0].shape[1]
    bias_part = tri_rows.astype(jnp.float32)
    usable = jnp.arange(extent, dtype=jnp.int32) < valid_length

    def one_block(inputs):
        run_block, total_block, sum_block, query_block, piece_block = inputs
        key_block = project(piece_block[0], pair_proj[1])
        value_block = project(piece_block[0], pair_proj[2])
        key_block = key_block.reshape(block_rows, extent, PAIR_HEADS, PAIR_HEAD_DIM)
        value_block = value_block.reshape(block_rows, extent, PAIR_HEADS, PAIR_HEAD_DIM)
        scores = jnp.einsum(
            "ihjd,ikhd->ihjk", query_block, key_block, preferred_element_type=jnp.float32
        )
        scores = jnp.where(usable, scores * pair_scale + bias_part[None], masked_value)
        new_max = jnp.maximum(run_block, jnp.max(scores, axis=-1))
        exponent = jnp.where(usable, jnp.exp(scores - new_max[..., None]), 0.0)
        factor = jnp.exp(run_block - new_max)
        new_total = total_block * factor + jnp.sum(exponent, axis=-1)
        product = jnp.einsum(
            "ihjk,ikhd->ihjd",
            exponent.astype(jnp.bfloat16),
            value_block,
            preferred_element_type=jnp.float32,
        )
        new_sum = sum_block * factor[..., None] + product
        return (new_max, new_total, new_sum)

    results = lax.map(
        one_block,
        (
            regroup(running),
            regroup(totals),
            regroup(summed),
            regroup(queries),
            tuple((regroup(item) for item in pieces)),
        ),
    )
    running, totals, summed = tuple(
        (result.reshape((rows_here,) + result.shape[2:]) for result in results)
    )
    attended = summed / totals[..., None]
    attended = jnp.transpose(attended, (0, 2, 1, 3)).reshape(rows_here, cols_here, channels)
    hidden = (gating * attended).astype(jnp.bfloat16)
    pair_out = (
        pair_rep.astype(jnp.float32)
        + jnp.dot(hidden, pair_out_weight, preferred_element_type=jnp.float32)
    ).astype(jnp.bfloat16)
    bias_normed = normalize(pair_out, bias_norm_gain)
    pair_bias = jnp.einsum(
        "rcd,dh->hrc", bias_normed, single_bias_weight, preferred_element_type=jnp.float32
    ).astype(jnp.bfloat16)
    head_bias = lax.all_to_all(pair_bias, "col", split_axis=0, concat_axis=2, tiled=True)
    single_normed = normalize(single_rep, single_gain)
    row_start = lax.axis_index("row") * rows_here
    mine = lax.dynamic_slice_in_dim(single_normed, row_start, rows_here, 0)
    local_width = single_proj.shape[2]
    heads_here = local_width // SINGLE_HEAD_DIM
    s_query = project(mine, single_proj[0]).reshape(rows_here, heads_here, SINGLE_HEAD_DIM)
    s_key = project(single_normed, single_proj[1]).reshape(tokens, heads_here, SINGLE_HEAD_DIM)
    s_value = project(single_normed, single_proj[2]).reshape(tokens, heads_here, SINGLE_HEAD_DIM)
    s_gate = jax.nn.sigmoid(jnp.dot(mine, single_proj[3], preferred_element_type=jnp.float32))
    scores = jnp.einsum(
        "ihd,jhd->hij", s_query, s_key, preferred_element_type=jnp.float32
    ) / math.sqrt(SINGLE_HEAD_DIM)
    scores = scores + head_bias.astype(jnp.float32)
    token_usable = jnp.arange(tokens, dtype=jnp.int32) < valid_length
    scores = jnp.where(token_usable, scores, masked_value)
    row_max = jnp.max(scores, axis=-1, keepdims=True)
    exponent = jnp.exp(scores - row_max)
    weights = (exponent / jnp.sum(exponent, axis=-1, keepdims=True)).astype(jnp.bfloat16)
    blended = jnp.einsum(
        "hij,jhd->ihd", weights, s_value, preferred_element_type=jnp.float32
    ).reshape(rows_here, local_width)
    s_hidden = (s_gate * blended).astype(jnp.bfloat16)
    partial_value = jnp.dot(s_hidden, single_out_weight, preferred_element_type=jnp.float32)
    reduced = lax.psum_scatter(
        partial_value.astype(jnp.bfloat16), "col", scatter_dimension=1, tiled=True
    ).astype(jnp.float32)
    col_start = lax.axis_index("col") * local_width
    residual = lax.dynamic_slice(single_rep, (row_start, col_start), (rows_here, local_width))
    single_out = (residual.astype(jnp.float32) + reduced).astype(jnp.bfloat16)
    return (pair_out, single_out)


def solution(mesh):
    in_specs = (
        P("row", "col", None),
        P(),
        P(),
        P(),
        P(),
        P(),
        P(),
        P(),
        P(None, None, "col"),
        P(),
        P(),
        P("col", None),
    )
    out_specs = (P("row", "col", None), P("row", "col"))
    return jax.shard_map(
        per_device, mesh=mesh, in_specs=in_specs, out_specs=out_specs, check_vma=False
    )
```

profile of v0, /device:TPU:0, one launch (start us, length us, event | category | flops | bytes accessed | tf_op | source)
XLA Modules:
  0.0 623.9 jit_solution(892850415658158468)
XLA Ops:
  15.1 45.7 %all_gather.10 = bf16[8,48,768]{1,0,2:T(8,128)(2,1)} all-gather(bf16[8,48,96]{1,0,2:T(8,128)(2,1)S(1)} %copy.27), channel_id=1, replica_groups=mesh['row'=16,'col'=8] {'col'}, dimensions={2}, use_global_device_ids=true | all-gather | bytes 663552 | tf_op jit(solution)/shard_map/all_gather | solution.py:49
  60.9 3.1 copy.28
  67.2 3.7 convolution_convert_fusion.2
  70.9 4.6 copy.26
  79.9 40.6 %all-gather.5.cloned.1.call-done = bf16[8,768,768]{2,0,1:T(8,128)(2,1)} async-done(((bf16[8,48,768]{2,0,1:T(8,128)(2,1)}), bf16[8,768,768]{2,0,1:T(8,128)(2,1)}) %all-gather.5.cloned.1.call-update) | async-done | bytes 9437200 | tf_op jit(solution)/shard_map/all_gather | solution.py:55
  122.7 206.2 %all-gather.3.cloned.1.call-done = bf16[48,768,256]{2,1,0:T(8,128)(2,1)} async-done(((bf16[48,96,256]{2,1,0:T(8,128)(2,1)}), bf16[48,768,256]{2,1,0:T(8,128)(2,1)}) %all-gather.3.cloned.1.call-update) | async-done | bytes 18874384 | tf_op jit(solution)/shard_map/all_gather | solution.py:64
  328.9 178.4 %while.13 = (s32[]{:T(128)}, f32[12,4,8,96]{3,2,1,0:T(8,128)S(1)}, f32[12,4,8,96,32]{3,4,2,1,0:T(8,128)}, bf16[12,4,8,96,32]{3,4,2,1,0:T(8,128)(2,1)}, bf16[12,4...) while((s32[]{:T(128)}, f32[12,4,8,96]{3,2,1,0:T(8,128)S(1)}, ...), condition=%wide.region_5.6_spmd.clone, body=%wide.region_2.5_spmd.clone.sunk | while | flops 1146732288 | bytes 46025852 | solution.py:92
  331.6 3.3 fusion.136
  334.9 3.0 fusion.137
  339.9 3.9 fusion.138
  346.5 3.3 fusion.136
  349.8 3.0 fusion.137
  354.8 3.9 fusion.138
  361.3 3.3 fusion.136
  364.6 3.0 fusion.137
  369.7 3.9 fusion.138
  376.2 3.3 fusion.136
  379.5 3.0 fusion.137
  384.5 3.9 fusion.138
  391.1 3.3 fusion.136
  399.4 3.9 fusion.138
  406.0 3.3 fusion.136
  409.2 3.0 fusion.137
  414.3 3.9 fusion.138
  420.8 3.3 fusion.136
  429.1 3.9 fusion.138
  435.7 3.3 fusion.136
  439.0 3.0 fusion.137
  444.0 3.9 fusion.138
  450.5 3.3 fusion.136
  453.8 3.0 fusion.137
  458.9 3.9 fusion.138
  465.4 3.3 fusion.136
  468.7 3.0 fusion.137
  473.7 3.9 fusion.138
  480.3 3.3 fusion.136
  483.6 3.0 fusion.137
  488.6 3.9 fusion.138
  495.1 3.3 fusion.136
  498.4 3.0 fusion.137
  503.4 3.9 fusion.138
  507.3 6.8 %bitcast_divide_fusion = f32[48,8,96,32]{2,3,1,0:T(8,128)} fusion(f32[12,4,8,96,32]{3,4,2,1,0:T(8,128)} %get-tuple-element.45, f32[48,8,96]{2,1,0:T(8,128)S(1)} %bitcast.133), kind=kLoop, calls=%fused_computation.38 | loop fusion | flops 1179648 | bytes 9584640 | tf_op jit(solution)/shard_map/div | solution.py:105
  514.2 6.3 %copy.31 = f32[48,96,256]{2,1,0:T(8,128)} copy(f32[48,96,256]{1,2,0:T(8,128)} %bitcast.126) | data formatting | bytes 9437184 | tf_op jit(solution)/shard_map/reshape | solution.py:106
  520.5 5.7 convert_reduce_fusion.1
  526.2 3.0 fusion.42
  532.8 3.4 all-to-all-start
  538.1 6.2 all-to-all-done
  547.4 67.7 %reduce-scatter.4.cloned.1.call-done = bf16[96,48]{1,0:T(8,128)(2,1)} async-done(((bf16[768,48]{1,0:T(8,128)(2,1)}), bf16[96,48]{1,0:T(8,128)(2,1)}) %reduce-scatter.4.cloned.1.call-update) | async-done | bytes 9232
  (142 shorter events, 90.1 us)
Async XLA Ops:
  7.2 538.2 %copy-start = (bf16[96,768]{1,0:T(8,128)(2,1)S(1)}, bf16[96,768]{1,0:T(8,128)(2,1)}, u32[]{:S(2)}) copy-start(bf16[96,768]{1,0:T(8,128)(2,1)} %param.25) | copy-start | bytes 442372
  7.2 5.8 copy-start.1
  7.2 5.7 copy-start.13
  7.2 5.7 copy-start.17
  7.2 113.3 %all-gather.5.cloned.1.call-start = ((), (), s32[]{:S(2)}) async-start(), calls=%async_computation.3 | async-start | bytes 10027008 | tf_op jit(solution)/shard_map/all_gather | solution.py:55
  10.0 54.2 %copy-start.7 = (f32[48,96]{1,0:T(8,128)}, f32[48,96]{1,0:T(8,128)S(1)}, u32[]{:S(2)}) copy-start(f32[48,96]{1,0:T(8,128)S(1)} %broadcast_multiply_fusion.1) | copy-start | bytes 55300
  13.0 51.2 %copy-start.10 = (f32[48,96]{1,0:T(8,128)}, f32[48,96]{1,0:T(8,128)S(1)}, u32[]{:S(2)}) copy-start(f32[48,96]{1,0:T(8,128)S(1)} %add_rsqrt_fusion.1) | copy-start | bytes 55300
  60.9 6.1 copy-start.6
  63.9 265.0 %all-gather.3.cloned.1.call-start = ((), (), s32[]{:S(2)}) async-start(), calls=%async_computation.2 | async-start | bytes 21233664 | tf_op jit(solution)/shard_map/all_gather | solution.py:64
  70.9 4.7 copy-start.4
  70.9 5.4 copy-start.12
  76.7 1.6 copy-start.3
  78.4 250.6 %copy-start.9 = (f32[12,4,8,96]{3,2,1,0:T(8,128)S(1)}, f32[12,4,8,96]{3,2,1,0:T(8,128)}, u32[]{:S(2)}) copy-start(f32[12,4,8,96]{3,2,1,0:T(8,128)} %custom-call) | copy-start | bytes 442372
  514.1 6.3 %copy-start.2 = (bf16[48,96,256]{2,1,0:T(8,128)(2,1)S(1)}, bf16[48,96,256]{2,1,0:T(8,128)(2,1)}, u32[]{:S(2)}) copy-start(bf16[48,96,256]{2,1,0:T(8,128)(2,1)} %param.14) | copy-start | bytes 7077892
  514.1 6.3 %copy-start.8 = (f32[48,96]{1,0:T(8,128)S(1)}, f32[48,96]{1,0:T(8,128)}, u32[]{:S(2)}) copy-start(f32[48,96]{1,0:T(8,128)} %copy-done.7) | copy-start | bytes 55300
  514.1 6.3 %copy-start.11 = (f32[48,96]{1,0:T(8,128)S(1)}, f32[48,96]{1,0:T(8,128)}, u32[]{:S(2)}) copy-start(f32[48,96]{1,0:T(8,128)} %copy-done.10) | copy-start | bytes 55300
  514.1 6.4 %copy-start.14 = (f32[256]{0:T(256)S(1)}, f32[256]{0:T(256)}, u32[]{:S(2)}) copy-start(f32[256]{0:T(256)} %param.17) | copy-start | bytes 3076
  514.1 6.4 %copy-start.15 = (bf16[256,256]{1,0:T(8,128)(2,1)S(1)}, bf16[256,256]{1,0:T(8,128)(2,1)}, u32[]{:S(2)}) copy-start(bf16[256,256]{1,0:T(8,128)(2,1)} %param.20) | copy-start | bytes 393220
  520.5 8.7 %copy-start.16 = (bf16[256,16]{0,1:T(8,128)(2,1)S(1)}, bf16[256,16]{0,1:T(8,128)(2,1)}, u32[]{:S(2)}) copy-start(bf16[256,16]{0,1:T(8,128)(2,1)} %param.24) | copy-start | bytes 24580
  520.5 8.7 %copy-start.18 = (f32[256]{0:T(256)S(1)}, f32[256]{0:T(256)}, u32[]{:S(2)}) copy-start(f32[256]{0:T(256)} %param.23) | copy-start | bytes 3076
  526.2 10.1 %copy-start.5 = (bf16[4,768,96]{1,2,0:T(8,128)(2,1)S(1)}, bf16[4,768,96]{1,2,0:T(8,128)(2,1)}, u32[]{:S(2)}) copy-start(bf16[4,768,96]{1,2,0:T(8,128)(2,1)} %param.22) | copy-start | bytes 1769476
  532.8 11.5 %all-to-all-start = ((bf16[16,48,96]{2,1,0:T(8,128)(2,1)}), bf16[16,48,96]{2,1,0:T(8,128)(2,1)S(1)}, u32[]{:S(2)}, u32[]{:S(2)}) async-start(bf16[16,48,96]{2,1,0:T(8,128)(2,1)} %copy.33), calls=%async_computation | async-start | bytes 393216 | tf_op jit(solution)/shard_map/all_to_all | solution.py:116
  536.2 78.9 %reduce-scatter.4.cloned.1.call-start = ((), (), s32[]{:S(2)}) async-start(), calls=%async_computation.4 | async-start | bytes 221184
Sparse Core Ops, SparseCore 0:
  64.1 56.4 all-gather.4
  122.8 206.0 all-gather.2
  547.5 67.5 reduce-scatter.3
where the time goes:
time: 626 us; the launch traced here: 624 us
  waiting for transfers between devices  321 us (51%)
  matrix products  154 us (25%)
  other arithmetic  66.1 us (11%)
  blocking collectives  45.7 us (7%)
  local copies, waits for them, and re-layouts  18 us (3%)
  between operations  14.8 us (2%)
    all_gather x1, waiting for transfers between devices, per_device(): pieces = (lax.all_gather(normed, 'col', axis=1, tiled=True),)  206 us
    unnamed x4, waiting for transfers between devices  67.8 us
    dot_general x28, matrix products, project(): jnp.dot(inputs, matrix, preferred_element_type=jnp.float32)  56.3 us
    dot_general x12, matrix products, one_block(): jnp.einsum('ihjk,ikhd->ihjd', exponent.astype(jnp.bfloat16), value_block,...  46.6 us
    all_gather x1, blocking collectives, per_device(): row_band = lax.all_gather(local_bias, 'col', axis=2, tiled=True)  45.7 us
    all_gather x1, waiting for transfers between devices, per_device(): bias_full = lax.all_gather(row_band, 'row', axis=1, tiled=True)  40.6 us
    dot_general x12, matrix products, one_block(): jnp.einsum('ihjd,ikhd->ihjk', query_block, key_block, preferred_element_t...  39.2 us
    reduce_sum x12, other arithmetic, one_block(): new_total = total_block * factor + jnp.sum(exponent, axis=-1)  35.6 us
  transfers between devices with their start and end apart: 4, of which 4 were waited for; matrix products, arithmetic and copies ran while one was open for 3% of the time, Pallas kernels for 0%

commit v1 on v0

v1 whole, which is shorter than its diff:
```python
import functools
import math

import jax
import jax.numpy as jnp
from jax import lax
from jax.experimental import pallas as pl
from jax.experimental.pallas import tpu as pltpu
from jax.sharding import Mesh, PartitionSpec as P

F32 = jnp.float32
BF16 = jnp.bfloat16
TOKENS = 768
CHANNELS = 256
HEADS = 8
HEAD_DIM = 32
SINGLE_DIM = 768
SINGLE_HEADS = 16
SINGLE_HEAD_DIM = 48
ROWS = 48
COLS = 96
MINE = 6
LOG2E = 1.4426950408889634
MASKED = -1e30
ROW = ("x", "zl", "core")
COL = ("y", "zh")
VMEM_LIMIT = 56 * 2**20


def params():
    return pltpu.CompilerParams(vmem_limit_bytes=VMEM_LIMIT)


def whole(shape):
    zeros = (0,) * len(shape)
    return pl.BlockSpec(shape, lambda *_: zeros)


def normalize(values, scales):
    floated = values.astype(F32)
    center = jnp.mean(floated, axis=-1, keepdims=True)
    moved = floated - center
    spread = jnp.mean(jnp.square(moved), axis=-1, keepdims=True)
    return (moved * lax.rsqrt(spread + 1e-05) * scales).astype(BF16)


def dot(a, b):
    return jnp.dot(a, b, preferred_element_type=F32)


def dot_nt(a, b):
    return lax.dot_general(a, b, (((1,), (1,)), ((), ())), preferred_element_type=F32)


def local_bias_kernel(limit_ref, pair_ref, gain_ref, weight_ref, out_ref, held):
    limit = limit_ref[0]
    key = lax.broadcasted_iota(jnp.int32, (HEADS, COLS), 1)

    def step(block, carry):
        start = block * 8
        normed = normalize(pair_ref[pl.ds(start, 8)].reshape(8 * COLS, CHANNELS), gain_ref[...])
        bias = dot_nt(weight_ref[...], normed) * LOG2E
        for row in range(8):
            piece = jnp.where(key < limit, bias[:HEADS, row * COLS : (row + 1) * COLS], MASKED)
            held[:, pl.ds(start + row, 1), :] = piece[:, None, :]
        return carry

    lax.fori_loop(0, ROWS // 8, step, 0)
    out_ref[...] = held[...].astype(BF16)


def local_bias(limit, pair, gain, weight):
    return pl.pallas_call(
        local_bias_kernel,
        grid_spec=pltpu.PrefetchScalarGridSpec(
            num_scalar_prefetch=1,
            grid=(1,),
            in_specs=[
                whole((ROWS, COLS, CHANNELS)),
                whole((1, CHANNELS)),
                whole((16, CHANNELS)),
            ],
            out_specs=whole((HEADS, ROWS, COLS)),
            scratch_shapes=[pltpu.VMEM((HEADS, ROWS, COLS), F32)],
        ),
        out_shape=jax.ShapeDtypeStruct((HEADS, ROWS, COLS), BF16),
        compiler_params=params(),
    )(limit, pair, gain, weight)


def join_kernel(in_ref, out_ref):
    out_ref[0] = jnp.concatenate([in_ref[col, 0] for col in range(8)], axis=1)


def join(pieces):
    return pl.pallas_call(
        join_kernel,
        grid=(4, 2),
        in_specs=[pl.BlockSpec((8, 1, 2 * ROWS, COLS), lambda h, z: (z, h, 0, 0))],
        out_specs=pl.BlockSpec((1, 2 * ROWS, TOKENS), lambda h, z: (h, z, 0)),
        out_shape=jax.ShapeDtypeStruct((4, 4 * ROWS, TOKENS), BF16),
        compiler_params=params(),
    )(pieces)


def project_kernel(pair_ref, gain_ref, wq_ref, wkt_ref, wv_ref, wg_ref, q_ref, kt_ref, v_ref, g_ref):
    normed = normalize(pair_ref[:, 0].reshape(TOKENS, CHANNELS), gain_ref[...])
    q_ref[0] = (dot(normed, wq_ref[...]) * (LOG2E / math.sqrt(HEAD_DIM))).astype(BF16)
    kt_ref[0] = dot_nt(wkt_ref[...], normed).astype(BF16)
    v_ref[0] = dot(normed, wv_ref[...]).astype(BF16)
    g_ref[0] = jax.nn.sigmoid(dot(normed, wg_ref[...])).astype(BF16)


def project(pair, gain, wq, wkt, wv, wg):
    square = whole((CHANNELS, CHANNELS))
    token = pl.BlockSpec((1, TOKENS, CHANNELS), lambda i: (i, 0, 0))
    token_shape = jax.ShapeDtypeStruct((MINE, TOKENS, CHANNELS), BF16)
    return pl.pallas_call(
        project_kernel,
        grid=(MINE,),
        in_specs=[
            pl.BlockSpec((8, 1, COLS, CHANNELS), lambda i: (0, i, 0, 0)),
            whole((1, CHANNELS)),
            square,
            square,
            square,
            square,
        ],
        out_specs=[token, pl.BlockSpec((1, CHANNELS, TOKENS), lambda i: (i, 0, 0)), token, token],
        out_shape=[
            token_shape,
            jax.ShapeDtypeStruct((MINE, CHANNELS, TOKENS), BF16),
            token_shape,
            token_shape,
        ],
        compiler_params=params(),
    )(pair, gain, wq, wkt, wv, wg)


def attend_kernel(place_ref, q_ref, kt_ref, v_ref, g_ref, pair_ref, first_ref, second_ref, wo_ref, *rest):
    out_ref = rest[-1]
    span = 4 * ROWS
    q = q_ref[0]
    kt = kt_ref[0]
    v = v_ref[0]
    ones = jnp.ones((TOKENS, 128), BF16)
    lane = lax.broadcasted_iota(jnp.int32, (1, CHANNELS), 1)
    half_lane = lax.broadcasted_iota(jnp.int32, (1, 128), 1)
    halves = []
    for half, bias_ref in enumerate((first_ref, second_ref)):
        values = jnp.concatenate([v[:, 128 * half : 128 * half + 128], ones], axis=1)
        total = jnp.zeros((span, 128), F32)
        for head in range(4):
            low = HEAD_DIM * (4 * half + head)
            own = jnp.where((lane >= low) & (lane < low + HEAD_DIM), q, jnp.zeros_like(q))
            scores = dot(own, kt) + bias_ref[head].astype(F32)
            top = jnp.max(scores, axis=1, keepdims=True)
            weights = jnp.exp2(scores - top).astype(BF16)
            mixed = dot(weights, values)
            mixed = mixed[:, :128] / mixed[:, 128:]
            low = HEAD_DIM * head
            total = jnp.where((half_lane >= low) & (half_lane < low + HEAD_DIM), mixed, total)
        halves.append(total)
    attended = jnp.concatenate(halves, axis=1)
    hidden = (g_ref[0].astype(F32) * attended).astype(BF16)
    result = pair_ref[:, 0].reshape(span, CHANNELS).astype(F32) + dot(hidden, wo_ref[...])
    out_ref[:, 0] = result.astype(BF16).reshape(2, COLS, CHANNELS)


def attend(place, q, kt, v, g, pair, first, second, wo, buffer):
    span = 4 * ROWS
    part = pl.BlockSpec((1, span, CHANNELS), lambda i, place: (i, place[0], 0))
    block = pl.BlockSpec((2, 1, COLS, CHANNELS), lambda i, place: (place[0], i, 0, 0))
    specs = [
        part,
        pl.BlockSpec((1, CHANNELS, TOKENS), lambda i, place: (i, 0, 0)),
        pl.BlockSpec((1, TOKENS, CHANNELS), lambda i, place: (i, 0, 0)),
        part,
        block,
        whole((4, span, TOKENS)),
        whole((4, span, TOKENS)),
        whole((CHANNELS, CHANNELS)),
    ]
    operands = [q, kt, v, g, pair, first, second, wo]
    aliases = {}
    if buffer is not None:
        specs.append(pl.BlockSpec(memory_space=pl.ANY))
        operands.append(buffer)
        aliases = {len(operands): 0}
    return pl.pallas_call(
        attend_kernel,
        grid_spec=pltpu.PrefetchScalarGridSpec(
            num_scalar_prefetch=1,
            grid=(MINE,),
            in_specs=specs,
            out_specs=block,
        ),
        out_shape=jax.ShapeDtypeStruct((8, MINE, COLS, CHANNELS), BF16),
        input_output_aliases=aliases,
        compiler_params=params(),
    )(place, *operands)


def single_project_kernel(start_ref, single_ref, gain_ref, weight_ref, kv_ref, qg_ref):
    normed = normalize(single_ref[...], gain_ref[...])
    kv_ref[0] = dot_nt(weight_ref[0], normed).astype(BF16)
    kv_ref[1] = dot_nt(weight_ref[1], normed).astype(BF16)
    start = pl.multiple_of(start_ref[0], 16)
    own = normalize(single_ref[pl.ds(start, ROWS)], gain_ref[...])
    qg_ref[0] = dot_nt(own, weight_ref[2]) * (LOG2E / math.sqrt(SINGLE_HEAD_DIM))
    qg_ref[1] = jax.nn.sigmoid(dot_nt(own, weight_ref[3]))


def single_project(start, single, gain, weight):
    return pl.pallas_call(
        single_project_kernel,
        grid_spec=pltpu.PrefetchScalarGridSpec(
            num_scalar_prefetch=1,
            grid=(1,),
            in_specs=[
                whole((TOKENS, SINGLE_DIM)),
                whole((1, SINGLE_DIM)),
                whole((4, COLS, SINGLE_DIM)),
            ],
            out_specs=[whole((2, COLS, TOKENS)), whole((2, ROWS, COLS))],
        ),
        out_shape=[
            jax.ShapeDtypeStruct((2, COLS, TOKENS), BF16),
            jax.ShapeDtypeStruct((2, ROWS, COLS), F32),
        ],
        compiler_params=params(),
    )(start, single, gain, weight)


def single_kernel(limit_ref, pair_ref, gain_ref, weight_ref, q_ref, g_ref, kt_ref, v_ref, wo_ref, rep_ref, out_ref):
    heads = SINGLE_HEADS
    biases = []
    for i in range(MINE):
        normed = normalize(pair_ref[:, i].reshape(TOKENS, CHANNELS), gain_ref[...])
        biases.append(dot_nt(weight_ref[...], normed).astype(BF16).astype(F32))
    bias = jnp.concatenate(biases, axis=0) * LOG2E
    channel = lax.broadcasted_iota(jnp.int32, (heads, SINGLE_DIM), 1)
    low = lax.broadcasted_iota(jnp.int32, (heads, SINGLE_DIM), 0) * SINGLE_HEAD_DIM
    inside = (channel >= low) & (channel < low + SINGLE_HEAD_DIM)
    spread = [
        jnp.where(inside, jnp.broadcast_to(q_ref[i : i + 1], (heads, SINGLE_DIM)), 0.0)
        for i in range(MINE)
    ]
    scores = dot(jnp.concatenate(spread, axis=0).astype(BF16), kt_ref[...]) + bias
    key = lax.broadcasted_iota(jnp.int32, (1, TOKENS), 1)
    scores = jnp.where(key < limit_ref[0], scores, MASKED)
    top = jnp.max(scores, axis=1, keepdims=True)
    exponent = jnp.exp2(scores - top)
    total = jnp.sum(exponent, axis=1, keepdims=True)
    mixed = dot((exponent / total).astype(BF16), v_ref[...])
    rows = [
        jnp.sum(jnp.where(inside, mixed[heads * i : heads * (i + 1)], 0.0), axis=0, keepdims=True)
        for i in range(MINE)
    ]
    hidden = (g_ref[...] * jnp.concatenate(rows, axis=0)).astype(BF16)
    out_ref[...] = (rep_ref[...].astype(F32) + dot(hidden, wo_ref[...])).astype(BF16)


def single_attend(limit, pair, gain, weight, q, g, kt, v, wo, rep):
    rows = whole((MINE, SINGLE_DIM))
    square = whole((SINGLE_DIM, SINGLE_DIM))
    return pl.pallas_call(
        single_kernel,
        grid_spec=pltpu.PrefetchScalarGridSpec(
            num_scalar_prefetch=1,
            grid=(1,),
            in_specs=[
                whole((8, MINE, COLS, CHANNELS)),
                whole((1, CHANNELS)),
                whole((SINGLE_HEADS, CHANNELS)),
                rows,
                rows,
                square,
                square,
                square,
                rows,
            ],
            out_specs=rows,
        ),
        out_shape=jax.ShapeDtypeStruct((MINE, SINGLE_DIM), BF16),
        compiler_params=params(),
    )(limit, pair, gain, weight, q, g, kt, v, wo, rep)


def exchange(value):
    return lax.all_to_all(value, COL, split_axis=0, concat_axis=0, tiled=True)


def shift(value, axis, by):
    size = lax.axis_size(axis)
    return lax.ppermute(value, axis, [(i, (i + by) % size) for i in range(size)])


def per_device(
    pair_rep,
    single_rep,
    length,
    pair_gain,
    pair_proj,
    bias_weight,
    pair_out_weight,
    single_gain,
    single_proj,
    bias_norm_gain,
    single_bias_weight,
    single_out_weight,
):
    core = lax.axis_index("core")
    x = lax.axis_index("x")
    row = lax.axis_index(ROW)
    col = lax.axis_index(COL)
    second_core = core == 1
    pair_gain = pair_gain.reshape(1, CHANNELS)

    pair = exchange(pair_rep.reshape(8, MINE, COLS, CHANNELS))

    limit = length - col * COLS
    weight = jnp.concatenate([bias_weight.T, jnp.zeros((8, CHANNELS), BF16)], axis=0)
    bias = local_bias(limit, pair_rep, pair_gain, weight)
    low, high = bias[:4], bias[4:]
    kept = jnp.where(second_core, high, low)
    given = jnp.where(second_core, low, high)
    taken = shift(given, "core", 1)
    block = jnp.where(second_core, jnp.stack([taken, kept], 1), jnp.stack([kept, taken], 1))
    copies = jnp.broadcast_to(block.reshape(1, 4, 2 * ROWS, COLS), (16, 4, 2 * ROWS, COLS))
    pieces = lax.all_to_all(copies, ("zl", "y", "zh"), split_axis=0, concat_axis=0, tiled=True)
    own = join(pieces)
    firsts = [own, shift(own, "x", 1), shift(own, "x", -1), shift(own, "x", 2)]
    seconds = [shift(item, "core", 1) for item in firsts]
    places = [x, (x + 3) % 4, (x + 1) % 4, (x + 2) % 4]

    single_t = jnp.swapaxes(single_proj, 1, 2)
    single_t = jnp.stack([single_t[1], single_t[2], single_t[0], single_t[3]])
    kv, qg = single_project(
        (row * ROWS).reshape(1), single_rep, single_gain.reshape(1, SINGLE_DIM), single_t
    )
    shared = jnp.concatenate([kv, single_out_weight[None]], axis=0)
    gathered = lax.all_gather(shared, COL, axis=0, tiled=False)
    qg = jnp.swapaxes(qg.reshape(2, 8, MINE, COLS), 0, 1)
    qg = jnp.transpose(exchange(qg), (1, 2, 0, 3)).reshape(2, MINE, SINGLE_DIM)
    single_kt = gathered[:, 0].reshape(SINGLE_DIM, TOKENS)
    single_v = gathered[:, 1].reshape(SINGLE_DIM, TOKENS).T
    single_wo = gathered[:, 2].reshape(SINGLE_DIM, SINGLE_DIM)

    turned = jnp.where(second_core, jnp.roll(pair_proj, 128, axis=2), pair_proj)
    wo = jnp.where(second_core, jnp.roll(pair_out_weight, 128, axis=0), pair_out_weight)
    q, kt, v, g = project(pair, pair_gain, turned[0], turned[1].T, turned[2], turned[3])

    buffer = None
    for place, first, second in zip(places, firsts, seconds):
        buffer = attend(place.reshape(1), q, kt, v, g, pair, first, second, wo, buffer)
    pair_out = exchange(buffer).reshape(ROWS, COLS, CHANNELS)

    rep = lax.dynamic_slice_in_dim(single_rep, row * ROWS + col * MINE, MINE, 0)
    rows = single_attend(
        length,
        buffer,
        bias_norm_gain.reshape(1, CHANNELS),
        single_bias_weight.T,
        qg[0],
        qg[1],
        single_kt,
        single_v,
        single_wo,
        rep,
    )
    rows = jnp.swapaxes(rows.reshape(MINE, 8, COLS), 0, 1)
    single_out = exchange(rows).reshape(ROWS, COLS)
    return pair_out, single_out


def solution(mesh):
    fine = Mesh(mesh.devices.reshape(4, 2, 2, 4, 2), ROW + COL)
    in_specs = (
        P(ROW, COL, None),
        P(),
        P(),
        P(),
        P(),
        P(),
        P(),
        P(),
        P(None, None, COL),
        P(),
        P(),
        P(COL, None),
    )
    out_specs = (P(ROW, COL, None), P(ROW, COL))
    return jax.shard_map(
        per_device, mesh=fine, in_specs=in_specs, out_specs=out_specs, check_vma=False
    )
```

time: 626 us -> 265 us (0.42)
  waiting for transfers between devices: 321 us -> 72.5 us
  matrix products: 154 us -> 0 us
  Pallas kernels: 0 us -> 89.6 us
  other arithmetic: 66.1 us -> 5.31 us
  starting transfers between devices: 3.69 us -> 23.7 us
  blocking collectives: 45.7 us -> 35.3 us
    all_gather x2 -> x1, waiting for transfers between devices: 247 us -> 0.01 us  [per_device(): gathered = lax.all_gather(shared, COL, axis=0, tiled=False)]
    dot_general x58 -> x0, matrix products: 154 us -> none  [the longest x28 56.3 us: project(): jnp.dot(inputs, matrix, preferred_element_type=jnp.float32)]
    pallas_call x0 -> x9, Pallas kernels: none -> 89.6 us  [the longest x4 60.2 us: attend(): pl.pallas_call(attend_kernel, grid_spec=pltpu.PrefetchScalarGridSpec(num_...]
    unnamed x4 -> x1, waiting for transfers between devices: 67.8 us -> 0.02 us
    all_gather x1 -> x0, blocking collectives: 45.7 us -> none  [per_device(): row_band = lax.all_gather(local_bias, 'col', axis=2, tiled=True)]
    ppermute x0 -> x8, waiting for transfers between devices: none -> 45.7 us  [shift(): lax.ppermute(value, axis, [(i, (i + by) % size) for i in range(size)])]
    reduce_sum x17 -> x0, other arithmetic: 44.9 us -> none  [the longest x12 35.6 us: one_block(): new_total = total_block * factor + jnp.sum(exponent, axis=-1)]
    all_to_all x0 -> x1, blocking collectives: none -> 35.3 us  [per_device(): lax.all_to_all(copies, ('zl', 'y', 'zh'), split_axis=0, concat_axis=0, ti...]
  transfers between devices with their start and end apart: 4 -> 13, of which waited for: 4 -> 6; matrix products, arithmetic and copies ran while one was open for 3% -> 8% of each run, Pallas kernels for 0% -> 33%
where the time goes in v1:
time: 265 us; the launch traced here: 264 us
  Pallas kernels  89.6 us (34%)
  waiting for transfers between devices  72.5 us (27%)
  blocking collectives  35.3 us (13%)
  starting transfers between devices  23.7 us (9%)
  local copies, waits for them, and re-layouts  22.2 us (8%)
  between operations  14.8 us (6%)
  other arithmetic  5.31 us (2%)
    pallas_call x4, Pallas kernels, attend(): pl.pallas_call(attend_kernel, grid_spec=pltpu.PrefetchScalarGridSpec(num_...  60.2 us
    ppermute x8, waiting for transfers between devices, shift(): lax.ppermute(value, axis, [(i, (i + by) % size) for i in range(size)])  45.7 us
    all_to_all x1, blocking collectives, per_device(): lax.all_to_all(copies, ('zl', 'y', 'zh'), split_axis=0, concat_axis=0, ti...  35.3 us
    all_to_all x4, waiting for transfers between devices, exchange(): return lax.all_to_all(value, COL, split_axis=0, concat_axis=0, tiled=True)  26.8 us
    all_to_all x4, starting transfers between devices, exchange(): return lax.all_to_all(value, COL, split_axis=0, concat_axis=0, tiled=True)  18.6 us
    pallas_call x1, Pallas kernels, project(): pl.pallas_call(project_kernel, grid=(MINE,), in_specs=[pl.BlockSpec((8, 1...  8.64 us
    pallas_call x1, Pallas kernels, single_attend(): pl.pallas_call(single_kernel, grid_spec=pltpu.PrefetchScalarGridSpec(num_...  5.95 us
    pallas_call x1, Pallas kernels, join(): pl.pallas_call(join_kernel, grid=(4, 2), in_specs=[pl.BlockSpec((8, 1, 2...  5.7 us
  transfers between devices with their start and end apart: 13, of which 6 were waited for; matrix products, arithmetic and copies ran while one was open for 8% of the time, Pallas kernels for 33%

profile of v1, /device:TPU:0, one launch (start us, length us, event | category | flops | bytes accessed | tf_op | source)
XLA Modules:
  0.0 263.5 jit_solution(16054971482597991052)
XLA Ops:
  7.2 1.0 fusion.1
  8.2 1.0 slice.86
  9.2 0.6 reshape.69.gain_ref
  9.8 0.9 pad_maximum_fusion.weight_ref
  10.7 3.5 %shard_map.138 = (bf16[2,96,768]{2,1,0:T(8,128)(2,1)}, f32[2,48,96]{2,1,0:T(8,128)}) custom-call(s32[1]{0:T(128)} %bitcast.19.start_ref, bf16[768,768]{1,0:T(8,128)(2,1)} %single_ref.1, f32[1,768]{1,0:T(1,128)} %reshape.69.gain_ref, bf16[4,96,768]{2,1,0:T(8,128)(2,1)} %pad_maximum_fusion.weight_ref), custom_call_target="tpu_custom_call" | custom-call | tf_op jit(solution)/shard_map/pallas_call | solution.py:215
  14.2 1.8 pad_maximum_fusion.1
  16.7 0.6 concatenate.15.weight_ref
  17.3 5.7 %shard_map.132 = bf16[8,48,96]{2,1,0:T(8,128)(2,1)} custom-call(s32[1]{0:T(128)S(6)} %sub.7.limit_ref, bf16[48,96,256]{2,1,0:T(8,128)(2,1)} %pair_ref.1, f32[1,256]{1,0:T(1,128)} %bitcast.58, bf16[16,256]{1,0:T(8,128)(2,1)} %concatenate.15.weight_ref), custom_call_target="tpu_custom_call" | custom-call | tf_op jit(solution)/shard_map/pallas_call | solution.py:73
  23.0 0.8 broadcast_select_fusion
  23.9 1.2 collective-permute-done
  25.2 0.3 broadcast_in_dim.4
  25.5 35.3 %all_to_all.25.in_ref = bf16[16,4,96,96]{3,2,1,0:T(8,128)(2,1)} all-to-all(bf16[16,4,96,96]{3,2,1,0:T(8,128)(2,1)S(1)} %broadcast_in_dim.4), channel_id=1, replica_groups=mesh['x'=4,'zl'=2,'core'=2,'y'=4,'zh'=2] {'zl','y','zh'}, dimensions={0} | all-to-all | bytes 2359296 | tf_op jit(solution)/shard_map/all_to_all | solution.py:331
  60.8 5.7 %shard_map.133.first_ref = bf16[4,192,768]{2,1,0:T(8,128)(2,1)} custom-call(bf16[16,4,96,96]{3,2,1,0:T(8,128)(2,1)} %all_to_all.25.in_ref), custom_call_target="tpu_custom_call" | custom-call | tf_op jit(solution)/shard_map/pallas_call | solution.py:96
  66.5 1.5 collective-permute-start.5
  67.9 1.8 collective-permute-start.3
  69.7 1.7 collective-permute-start.1
  71.5 3.8 %all-to-all-start = ((bf16[8,6,96,256]{3,2,1,0:T(8,128)(2,1)}), bf16[8,6,96,256]{3,2,1,0:T(8,128)(2,1)S(1)}, u32[]{:S(2)}, u32[]{:S(2)}) async-start(bf16[8,6,96,256]{3,2,1,0:T(8,128)(2,1)} %bitcast.44), calls=%async_computation | async-start | bytes 4718592 | tf_op jit(solution)/shard_map/all_to_all | solution.py:291
  75.2 1.5 copy.42
  76.7 19.2 %collective-permute-done.5.first_ref = bf16[4,192,768]{2,1,0:T(8,128)(2,1)} collective-permute-done((bf16[4,192,768]{2,1,0:T(8,128)(2,1)}, bf16[4,192,768]{2,1,0:T(8,128)(2,1)}, u32[]{:S(2)}, u32[]{:S(2)}) %collective-permute-start.5) | collective-permute-done | bytes 1179680 | tf_op jit(solution)/shard_map/ppermute | solution.py:296
  95.9 1.2 collective-permute-done.3.first_ref
  97.2 24.0 %collective-permute-done.1.first_ref = bf16[4,192,768]{2,1,0:T(8,128)(2,1)} collective-permute-done((bf16[4,192,768]{2,1,0:T(8,128)(2,1)}, bf16[4,192,768]{2,1,0:T(8,128)(2,1)}, u32[]{:S(2)}, u32[]{:S(2)}) %collective-permute-start.1) | collective-permute-done | bytes 1179680 | tf_op jit(solution)/shard_map/ppermute | solution.py:296
  121.2 1.5 fusion.3
  122.7 1.1 fusion.2
  123.8 0.1 maximum_select_fusion
  123.9 0.8 slice_bitcast_fusion
  124.8 4.1 %all-to-all-start.3 = ((f32[8,2,6,96]{3,1,2,0:T(2,128)}), f32[8,2,6,96]{3,1,2,0:T(2,128)}, u32[]{:S(2)}, u32[]{:S(2)}) async-start(f32[8,2,6,96]{3,1,2,0:T(2,128)} %bitcast.54), calls=%async_computation.3 | async-start | bytes 98304 | tf_op jit(solution)/shard_map/all_to_all | solution.py:291
  128.9 1.6 maximum_select_fusion.1.wo_ref
  130.5 1.6 copy.40.wkt_ref
  132.2 8.6 %shard_map.131 = (bf16[6,768,256]{2,1,0:T(8,128)(2,1)}, bf16[6,256,768]{2,1,0:T(8,128)(2,1)}, bf16[6,768,256]{2,1,0:T(8,128)(2,1)}, bf16[6,768,256]{2,1,0:T(8,128)(2,1)}) custom-call(bf16[8,6,96,256]{3,2,1,0:T(8,128)(2,1)} %copy-done, f32[1,256]{1,0:T(1,128)} %bitcast.59, bf16[256,256]{1,0:T(8,128)(2,1)} %get-tuple-element.22.wq_ref, ...), custom_call_target="tpu_custom_call" | custom-call | tf_op jit(solution)/shard_map/pallas_call | solution.py:118
  140.8 15.0 %shard_map.134.rest_0_ = bf16[8,6,96,256]{3,2,1,0:T(8,128)(2,1)} custom-call(s32[1]{0:T(128)} %bitcast.15.place_ref, bf16[6,768,256]{2,1,0:T(8,128)(2,1)} %get-tuple-element.8.q_ref, bf16[6,256,768]{2,1,0:T(8,128)(2,1)} %get-tuple-element.9.kt_ref, bf16[6,768,256]{2,1,0:T(8,128)(2,1)} %get-tuple-element.10.v_ref, ...), custom_call_target="tpu_custom_call" | custom-call | tf_op jit(solution)/shard_map/pallas_call | solution.py:190
  155.9 15.0 %shard_map.135.rest_0_ = bf16[8,6,96,256]{3,2,1,0:T(8,128)(2,1)} custom-call(s32[1]{0:T(128)} %bitcast.14.place_ref, bf16[6,768,256]{2,1,0:T(8,128)(2,1)} %get-tuple-element.8.q_ref, bf16[6,256,768]{2,1,0:T(8,128)(2,1)} %get-tuple-element.9.kt_ref, bf16[6,768,256]{2,1,0:T(8,128)(2,1)} %get-tuple-element.10.v_ref, ...), custom_call_target="tpu_custom_call", output_to_operand_aliasing={{}: (9, {})} | custom-call | tf_op jit(solution)/shard_map/pallas_call | solution.py:190
  170.9 15.0 %shard_map.136.rest_0_ = bf16[8,6,96,256]{3,2,1,0:T(8,128)(2,1)} custom-call(s32[1]{0:T(128)} %bitcast.13.place_ref, bf16[6,768,256]{2,1,0:T(8,128)(2,1)} %get-tuple-element.8.q_ref, bf16[6,256,768]{2,1,0:T(8,128)(2,1)} %get-tuple-element.9.kt_ref, bf16[6,768,256]{2,1,0:T(8,128)(2,1)} %get-tuple-element.10.v_ref, ...), custom_call_target="tpu_custom_call", output_to_operand_aliasing={{}: (9, {})} | custom-call | tf_op jit(solution)/shard_map/pallas_call | solution.py:190
  185.9 15.1 %shard_map.137.pair_ref = bf16[8,6,96,256]{3,2,1,0:T(8,128)(2,1)} custom-call(s32[1]{0:T(128)} %bitcast.place_ref, bf16[6,768,256]{2,1,0:T(8,128)(2,1)} %get-tuple-element.8.q_ref, bf16[6,256,768]{2,1,0:T(8,128)(2,1)} %get-tuple-element.9.kt_ref, bf16[6,768,256]{2,1,0:T(8,128)(2,1)} %get-tuple-element.10.v_ref, ...), custom_call_target="tpu_custom_call", output_to_operand_aliasing={{}: (9, {})} | custom-call | tf_op jit(solution)/shard_map/pallas_call | solution.py:190
  201.0 6.9 %all-to-all-start.2 = ((bf16[8,6,96,256]{3,2,1,0:T(8,128)(2,1)}), bf16[8,6,96,256]{3,2,1,0:T(8,128)(2,1)S(1)}, u32[]{:S(2)}, u32[]{:S(2)}) async-start(bf16[8,6,96,256]{3,2,1,0:T(8,128)(2,1)} %shard_map.137.pair_ref), calls=%async_computation.2 | async-start | bytes 4718592 | tf_op jit(solution)/shard_map/all_to_all | solution.py:291
  207.9 1.3 constant_dynamic-slice_fusion.rep_ref
  209.3 0.9 fusion.4
  210.2 0.7 squeeze.22.q_ref
  210.9 0.7 squeeze.23.g_ref
  211.6 3.6 %fusion = (bf16[8,1,96,768]{3,2,1,0:T(8,128)(2,1)}, bf16[8,1,96,768]{3,2,1,0:T(8,128)(2,1)S(1)}, bf16[8,1,96,768]{3,2,1,0:T(8,128)(2,1)}) fusion(bf16[8,3,96,768]{3,2,1,0:T(8,128)(2,1)} %bitcast.50), kind=kLoop, calls=%fused_computation.13 | loop fusion | bytes 7077888 | tf_op jit(solution)/shard_map/slice | solution.py:348
  215.2 1.5 copy.45
  216.7 5.9 %shard_map.139 = bf16[6,768]{1,0:T(8,128)(2,1)} custom-call(s32[1]{0:T(128)S(6)} %copy.53.limit_ref, bf16[8,6,96,256]{3,2,1,0:T(8,128)(2,1)} %shard_map.137.pair_ref, f32[1,256]{1,0:T(1,128)} %bitcast.61, bf16[16,256]{1,0:T(8,128)(2,1)} %bitcast.57, f32[6,768]{1,0:T(8,128)} %squeeze.22.q_ref, f32[6,768]{1,0:T(8,128)} %squeeze.23.g_ref, ...), custom_call_target="tpu_custom_call" | custom-call | tf_op jit(solution)/shard_map/pallas_call | solution.py:267
  222.6 0.8 reshape.71
  223.4 0.6 copy.48
  224.0 19.1 %all-to-all-done.2 = bf16[8,6,96,256]{3,2,1,0:T(8,128)(2,1)S(1)} async-done(((bf16[8,6,96,256]{3,2,1,0:T(8,128)(2,1)}), bf16[8,6,96,256]{3,2,1,0:T(8,128)(2,1)S(1)}, u32[]{:S(2)}, u32[]{:S(2)}) %all-to-all-start.2) | async-done | bytes 2359328 | tf_op jit(solution)/shard_map/all_to_all | solution.py:291
  243.2 3.8 %all-to-all-start.4 = ((bf16[8,6,96]{2,1,0:T(8,128)(2,1)}), bf16[8,6,96]{2,1,0:T(8,128)(2,1)S(1)}, u32[]{:S(2)}, u32[]{:S(2)}) async-start(bf16[8,6,96]{2,1,0:T(8,128)(2,1)} %bitcast.43), calls=%async_computation.4 | async-start | bytes 32768 | tf_op jit(solution)/shard_map/all_to_all | solution.py:291
  247.0 7.7 %all-to-all-done.4 = bf16[8,6,96]{2,1,0:T(8,128)(2,1)S(1)} async-done(((bf16[8,6,96]{2,1,0:T(8,128)(2,1)}), bf16[8,6,96]{2,1,0:T(8,128)(2,1)S(1)}, u32[]{:S(2)}, u32[]{:S(2)}) %all-to-all-start.4) | async-done | bytes 9248 | tf_op jit(solution)/shard_map/all_to_all | solution.py:291
  254.7 0.6 reshape.72
  255.3 1.4 copy.54
  (30 shorter events, 0.2 us)
Async XLA Ops:
  7.2 2.1 copy-start.5
  7.2 204.4 %all-gather.3.cloned.1.call-start = ((), (), s32[]{:S(2)}) async-start(), calls=%async_computation.5 | async-start | bytes 3981312 | tf_op jit(solution)/shard_map/all_gather | solution.py:343
  10.7 3.5 %copy-start.3 = (bf16[96,768]{1,0:T(8,128)(2,1)S(1)}, bf16[96,768]{1,0:T(8,128)(2,1)}, u32[]{:S(2)}) copy-start(bf16[96,768]{1,0:T(8,128)(2,1)} %param.23) | copy-start | bytes 442372
  10.7 6.0 %copy-start.4 = (bf16[256,8]{0,1:T(8,128)(2,1)S(1)}, bf16[256,8]{0,1:T(8,128)(2,1)}, u32[]{:S(2)}) copy-start(bf16[256,8]{0,1:T(8,128)(2,1)} %param.17) | copy-start | bytes 12292
  23.8 1.3 collective-permute-start
  66.5 29.4 %collective-permute-start.5 = (bf16[4,192,768]{2,1,0:T(8,128)(2,1)}, bf16[4,192,768]{2,1,0:T(8,128)(2,1)}, u32[]{:S(2)}, u32[]{:S(2)}) collective-permute-start(bf16[4,192,768]{2,1,0:T(8,128)(2,1)} %shard_map.133.first_ref), channel_id=1, source_target_pairs={{0,32},{32,64},{64,96},{96,0},{1,33},{33,65},{65,97},{97,1},{2,34}... | collective-permute-start | bytes 3538952 | tf_op jit(solution)/shard_map/ppermute | solution.py:296
  67.9 29.2 %collective-permute-start.3 = (bf16[4,192,768]{2,1,0:T(8,128)(2,1)}, bf16[4,192,768]{2,1,0:T(8,128)(2,1)}, u32[]{:S(2)}, u32[]{:S(2)}) collective-permute-start(bf16[4,192,768]{2,1,0:T(8,128)(2,1)} %shard_map.133.first_ref), channel_id=1, source_target_pairs={{0,96},{32,0},{64,32},{96,64},{1,97},{33,1},{65,33},{97,65},{2,98}... | collective-permute-start | bytes 3538952 | tf_op jit(solution)/shard_map/ppermute | solution.py:296
  69.7 51.5 %collective-permute-start.1 = (bf16[4,192,768]{2,1,0:T(8,128)(2,1)}, bf16[4,192,768]{2,1,0:T(8,128)(2,1)}, u32[]{:S(2)}, u32[]{:S(2)}) collective-permute-start(bf16[4,192,768]{2,1,0:T(8,128)(2,1)} %shard_map.133.first_ref), channel_id=1, source_target_pairs={{0,64},{32,96},{64,0},{96,32},{1,65},{33,97},{65,1},{97,33},{2,66}... | collective-permute-start | bytes 3538952 | tf_op jit(solution)/shard_map/ppermute | solution.py:296
  71.5 5.3 %copy-start.1 = (bf16[4,192,768]{2,1,0:T(8,128)(2,1)S(1)}, bf16[4,192,768]{2,1,0:T(8,128)(2,1)}, u32[]{:S(2)}) copy-start(bf16[4,192,768]{2,1,0:T(8,128)(2,1)} %shard_map.133.first_ref) | copy-start | bytes 3538948
  71.5 53.3 %all-to-all-start = ((bf16[8,6,96,256]{3,2,1,0:T(8,128)(2,1)}), bf16[8,6,96,256]{3,2,1,0:T(8,128)(2,1)S(1)}, u32[]{:S(2)}, u32[]{:S(2)}) async-start(bf16[8,6,96,256]{3,2,1,0:T(8,128)(2,1)} %bitcast.44), calls=%async_computation | async-start | bytes 4718592 | tf_op jit(solution)/shard_map/all_to_all | solution.py:291
  75.2 48.6 %copy-start.2 = (bf16[4,256,256]{2,1,0:T(8,128)(2,1)S(1)}, bf16[4,256,256]{2,1,0:T(8,128)(2,1)}, u32[]{:S(2)}) copy-start(bf16[4,256,256]{2,1,0:T(8,128)(2,1)} %param.16) | copy-start | bytes 1572868
  76.7 64.1 %collective-permute-start.7 = (bf16[4,192,768]{2,1,0:T(8,128)(2,1)S(1)}, bf16[4,192,768]{2,1,0:T(8,128)(2,1)}, u32[]{:S(2)}, u32[]{:S(2)}) collective-permute-start(bf16[4,192,768]{2,1,0:T(8,128)(2,1)S(1)} %copy-done.1), channel_id=1, source_target_pairs={{0,8},{8,0},{1,9},{9,1},{2,10},{10,2},{3,11},{11,3},{4,12},{12,4},... | collective-permute-start | bytes 3538952 | tf_op jit(solution)/shard_map/ppermute | solution.py:296
  95.9 60.0 %collective-permute-start.6 = (bf16[4,192,768]{2,1,0:T(8,128)(2,1)}, bf16[4,192,768]{2,1,0:T(8,128)(2,1)}, u32[]{:S(2)}, u32[]{:S(2)}) collective-permute-start(bf16[4,192,768]{2,1,0:T(8,128)(2,1)} %collective-permute-done.5.first_ref), channel_id=1, source_target_pairs={{0,8},{8,0},{1,9},{9,1},{2,10},{10,2},{3,11},{11,3},{4,12},{12,4},... | collective-permute-start | bytes 3538952 | tf_op jit(solution)/shard_map/ppermute | solution.py:296
  97.2 73.7 %collective-permute-start.4 = (bf16[4,192,768]{2,1,0:T(8,128)(2,1)}, bf16[4,192,768]{2,1,0:T(8,128)(2,1)}, u32[]{:S(2)}, u32[]{:S(2)}) collective-permute-start(bf16[4,192,768]{2,1,0:T(8,128)(2,1)} %collective-permute-done.3.first_ref), channel_id=1, source_target_pairs={{0,8},{8,0},{1,9},{9,1},{2,10},{10,2},{3,11},{11,3},{4,12},{12,4},... | collective-permute-start | bytes 3538952 | tf_op jit(solution)/shard_map/ppermute | solution.py:296
  121.2 64.7 %collective-permute-start.2 = (bf16[4,192,768]{2,1,0:T(8,128)(2,1)}, bf16[4,192,768]{2,1,0:T(8,128)(2,1)}, u32[]{:S(2)}, u32[]{:S(2)}) collective-permute-start(bf16[4,192,768]{2,1,0:T(8,128)(2,1)} %collective-permute-done.1.first_ref), channel_id=1, source_target_pairs={{0,8},{8,0},{1,9},{9,1},{2,10},{10,2},{3,11},{11,3},{4,12},{12,4},... | collective-permute-start | bytes 3538952 | tf_op jit(solution)/shard_map/ppermute | solution.py:296
  124.8 7.4 %copy-start = (bf16[8,6,96,256]{3,2,1,0:T(8,128)(2,1)}, bf16[8,6,96,256]{3,2,1,0:T(8,128)(2,1)S(1)}, u32[]{:S(2)}) copy-start(bf16[8,6,96,256]{3,2,1,0:T(8,128)(2,1)S(1)} %all-to-all-done.pair_ref) | copy-start | bytes 7077892
  124.8 76.2 %all-to-all-start.3 = ((f32[8,2,6,96]{3,1,2,0:T(2,128)}), f32[8,2,6,96]{3,1,2,0:T(2,128)}, u32[]{:S(2)}, u32[]{:S(2)}) async-start(f32[8,2,6,96]{3,1,2,0:T(2,128)} %bitcast.54), calls=%async_computation.3 | async-start | bytes 98304 | tf_op jit(solution)/shard_map/all_to_all | solution.py:291
  201.0 42.2 %all-to-all-start.2 = ((bf16[8,6,96,256]{3,2,1,0:T(8,128)(2,1)}), bf16[8,6,96,256]{3,2,1,0:T(8,128)(2,1)S(1)}, u32[]{:S(2)}, u32[]{:S(2)}) async-start(bf16[8,6,96,256]{3,2,1,0:T(8,128)(2,1)} %shard_map.137.pair_ref), calls=%async_computation.2 | async-start | bytes 4718592 | tf_op jit(solution)/shard_map/all_to_all | solution.py:291
  243.2 11.5 %all-to-all-start.4 = ((bf16[8,6,96]{2,1,0:T(8,128)(2,1)}), bf16[8,6,96]{2,1,0:T(8,128)(2,1)S(1)}, u32[]{:S(2)}, u32[]{:S(2)}) async-start(bf16[8,6,96]{2,1,0:T(8,128)(2,1)} %bitcast.43), calls=%async_computation.4 | async-start | bytes 32768 | tf_op jit(solution)/shard_map/all_to_all | solution.py:291
Sparse Core Ops, SparseCore 0:
  16.1 98.2 all-gather.2

commit v2 on v1

v2 whole, which is shorter than its diff:
```python
import functools
import math

import jax
import jax.numpy as jnp
from jax import lax
from jax.experimental import pallas as pl
from jax.experimental.pallas import tpu as pltpu
from jax.sharding import Mesh, PartitionSpec as P

F32 = jnp.float32
BF16 = jnp.bfloat16
TOKENS = 768
CHANNELS = 256
HEADS = 8
HEAD_DIM = 32
SINGLE_DIM = 768
SINGLE_HEADS = 16
SINGLE_HEAD_DIM = 48
ROWS = 48
COLS = 96
MINE = 6
LOG2E = 1.4426950408889634
MASKED = -1e30
ROW = ("x", "zl", "core")
COL = ("y", "zh")
VMEM_LIMIT = 56 * 2**20


def params():
    return pltpu.CompilerParams(vmem_limit_bytes=VMEM_LIMIT)


def cost(time):
    return pl.CostEstimate(flops=time * 10000000, bytes_accessed=time * 30000, transcendentals=0)


def whole(shape):
    zeros = (0,) * len(shape)
    return pl.BlockSpec(shape, lambda *_: zeros)


def normalize(values, scales):
    floated = values.astype(F32)
    center = jnp.mean(floated, axis=-1, keepdims=True)
    moved = floated - center
    spread = jnp.mean(jnp.square(moved), axis=-1, keepdims=True)
    return (moved * lax.rsqrt(spread + 1e-05) * scales).astype(BF16)


def dot(a, b):
    return jnp.dot(a, b, preferred_element_type=F32)


def dot_nt(a, b):
    return lax.dot_general(a, b, (((1,), (1,)), ((), ())), preferred_element_type=F32)


def local_bias_kernel(limit_ref, pair_ref, gain_ref, weight_ref, out_ref, held):
    limit = limit_ref[0]
    key = lax.broadcasted_iota(jnp.int32, (HEADS, COLS), 1)
    weight = weight_ref[...]

    def step(block, carry):
        start = block * 8
        normed = normalize(pair_ref[pl.ds(start, 8)].reshape(8 * COLS, CHANNELS), gain_ref[...])
        bias = dot_nt(weight, normed) * LOG2E
        for row in range(8):
            piece = jnp.where(key < limit, bias[:, row * COLS : (row + 1) * COLS], MASKED)
            held[:, pl.ds(start + row, 1), :] = piece[:, None, :]
        return carry

    lax.fori_loop(0, ROWS // 8, step, 0)
    for half in range(2):
        out_ref[half] = jnp.concatenate([held[4 * half + h] for h in range(4)], axis=1).astype(BF16)


def local_bias(limit, pair, gain, weight):
    return pl.pallas_call(
        local_bias_kernel,
        grid_spec=pltpu.PrefetchScalarGridSpec(
            num_scalar_prefetch=1,
            grid=(1,),
            in_specs=[
                whole((ROWS, COLS, CHANNELS)),
                whole((1, CHANNELS)),
                whole((HEADS, CHANNELS)),
            ],
            out_specs=whole((2, ROWS, 4 * COLS)),
            scratch_shapes=[pltpu.VMEM((HEADS, ROWS, COLS), F32)],
        ),
        out_shape=jax.ShapeDtypeStruct((2, ROWS, 4 * COLS), BF16),
        compiler_params=params(),
        cost_estimate=cost(5),
    )(limit, pair, gain, weight)


def join_kernel(place_ref, a_ref, b_ref, c_ref, d_ref, o0_ref, o1_ref, held):
    y = place_ref[0]
    z = place_ref[1]
    for slot, ref in enumerate((a_ref, b_ref, c_ref, d_ref)):
        held[slot] = ref[...]
    for low in range(2):
        for core in range(2):
            blocks = []
            for col in range(8):
                depth = lax.rem(2 * (col % 2) + low - z + 4, 4)
                side = lax.rem(col // 2 - y + 4, 4)
                blocks.append(held[depth, side, core])
            for head in range(4):
                line = jnp.concatenate([b[:, COLS * head : COLS * (head + 1)] for b in blocks], axis=1)
                at = 2 * low + core
                o0_ref[head, 16 * at : 16 * (at + 1)] = line[32:]
                o1_ref[head, 32 * at : 32 * (at + 1)] = line[:32]


def join(place, pieces):
    shape = (4, 2, ROWS, 4 * COLS)
    outs = [(4, 4 * rows, TOKENS) for rows in (16, 32)]
    return pl.pallas_call(
        join_kernel,
        grid_spec=pltpu.PrefetchScalarGridSpec(
            num_scalar_prefetch=1,
            grid=(1,),
            in_specs=[whole(shape)] * 4,
            out_specs=[whole(out) for out in outs],
            scratch_shapes=[pltpu.VMEM((4,) + shape, BF16)],
        ),
        out_shape=[jax.ShapeDtypeStruct(out, BF16) for out in outs],
        compiler_params=params(),
        cost_estimate=cost(3),
    )(place, *pieces)


def project_kernel(pair_ref, gain_ref, wq_ref, wkt_ref, wv_ref, wg_ref, *rest):
    kt_ref, v_ref, q0_ref, q1_ref, g0_ref, g1_ref, old0_ref, old1_ref = rest[-8:]
    old = pair_ref[...].reshape(TOKENS, CHANNELS)
    normed = normalize(old, gain_ref[...])
    q = (dot(normed, wq_ref[...]) * (LOG2E / math.sqrt(HEAD_DIM))).astype(BF16)
    kt_ref[0] = dot_nt(wkt_ref[...], normed).astype(BF16)
    v_ref[0] = dot(normed, wv_ref[...]).astype(BF16)
    g = jax.nn.sigmoid(dot(normed, wg_ref[...])).astype(BF16)
    for value, ref0, ref1 in ((q, q0_ref, q1_ref), (g, g0_ref, g1_ref), (old, old0_ref, old1_ref)):
        value = value.reshape(16, ROWS, CHANNELS)
        ref0[0] = value[:, 32:].reshape(4, 64, CHANNELS)
        ref1[0] = value[:, :32].reshape(4, 128, CHANNELS)


def project(pair, gain, wq, wkt, wv, wg, start, buffers):
    square = whole((CHANNELS, CHANNELS))
    blocks = [(CHANNELS, TOKENS), (TOKENS, CHANNELS)] + [(4, 64, CHANNELS), (4, 128, CHANNELS)] * 3
    operands = [pair, gain, wq, wkt, wv, wg]
    aliases = {len(operands) + n: n for n in range(len(buffers))}

    def spec(block):
        zeros = (0,) * len(block)
        return pl.BlockSpec((1,) + block, lambda i: (start + i,) + zeros)

    return pl.pallas_call(
        project_kernel,
        grid=(MINE // 2,),
        in_specs=[
            pl.BlockSpec((8, 6, 16, CHANNELS), lambda i: (0, i, 0, 0)),
            whole((1, CHANNELS)),
            square,
            square,
            square,
            square,
        ]
        + [pl.BlockSpec(memory_space=pl.ANY)] * len(buffers),
        out_specs=[spec(block) for block in blocks],
        out_shape=[jax.ShapeDtypeStruct((MINE,) + block, BF16) for block in blocks],
        input_output_aliases=aliases,
        compiler_params=params(),
        cost_estimate=cost(5),
    )(*operands, *buffers)


def attend_chunk(order, span, q_ref, g_ref, old_ref, firsts, seconds, kt, v, wo):
    q = jnp.concatenate([q_ref[0, at] for at in order], axis=0)
    ones = jnp.ones((TOKENS, 128), BF16)
    lane = lax.broadcasted_iota(jnp.int32, (1, CHANNELS), 1)
    half_lane = lax.broadcasted_iota(jnp.int32, (1, 128), 1)
    halves = []
    for half, refs in enumerate((firsts, seconds)):
        values = jnp.concatenate([v[:, 128 * half : 128 * half + 128], ones], axis=1)
        total = jnp.zeros((4 * span, 128), F32)
        for head in range(4):
            low = HEAD_DIM * (4 * half + head)
            own = jnp.where((lane >= low) & (lane < low + HEAD_DIM), q, jnp.zeros_like(q))
            bias = jnp.concatenate([ref[head] for ref in refs], axis=0)
            scores = dot(own, kt) + bias.astype(F32)
            top = jnp.max(scores, axis=1, keepdims=True)
            weights = jnp.exp2(scores - top).astype(BF16)
            mixed = dot(weights, values)
            mixed = mixed[:, :128] / mixed[:, 128:]
            low = HEAD_DIM * head
            total = jnp.where((half_lane >= low) & (half_lane < low + HEAD_DIM), mixed, total)
        halves.append(total)
    attended = jnp.concatenate(halves, axis=1)
    g = jnp.concatenate([g_ref[0, at] for at in order], axis=0)
    update = dot((g.astype(F32) * attended).astype(BF16), wo)
    return [
        (old_ref[0, at].astype(F32) + update[span * step : span * (step + 1)]).astype(BF16)
        for step, at in enumerate(order)
    ]


def attend_kernel(x_ref, kt_ref, v_ref, wo_ref, q_ref, g_ref, old_ref, *rest):
    out_ref = rest[-1]
    order = [lax.rem(x_ref[0] + step, 4) for step in range(4)]
    span = q_ref.shape[2]
    parts = attend_chunk(
        order, span, q_ref, g_ref, old_ref, rest[:4], rest[4:8], kt_ref[0], v_ref[0], wo_ref[...]
    )
    for at, part in zip(order, parts):
        out_ref[pl.ds(2 * at, 2), 0] = part.reshape(2, 2, span // 4, CHANNELS)


def attend_late_kernel(x_ref, kt_ref, v_ref, wo_ref, q0_ref, g0_ref, old0_ref, q1_ref, g1_ref, old1_ref, *rest):
    out_ref = rest[-1]
    order = [lax.rem(x_ref[0] + step, 4) for step in range(4)]
    chunks = ((q0_ref, g0_ref, old0_ref, rest[:8]), (q1_ref, g1_ref, old1_ref, rest[8:16]))
    for chunk, (q_ref, g_ref, old_ref, bias) in enumerate(chunks):
        span = q_ref.shape[2]
        parts = attend_chunk(
            order, span, q_ref, g_ref, old_ref, bias[:4], bias[4:], kt_ref[0], v_ref[0], wo_ref[...]
        )
        count = chunk + 1
        for at, part in zip(order, parts):
            part = part.reshape(2, 2, count, 16, CHANNELS)
            for core in range(2):
                first = 3 * core + (2 if chunk == 0 else 0)
                out_ref[pl.ds(2 * at, 2), first : first + count] = part[:, core]


def attend(x, kt, v, wo, chunks, rows, start, out_block, out_index, out_shape, buffer, time):
    def spec(shape):
        zeros = (0,) * len(shape)
        return pl.BlockSpec((1,) + shape, lambda i, x: (start + i,) + zeros)

    operands = [x, kt, v, wo]
    specs = [spec((CHANNELS, TOKENS)), spec((TOKENS, CHANNELS)), whole((CHANNELS, CHANNELS))]
    for tokens, _ in chunks:
        operands += tokens
        specs += [spec(token.shape[1:]) for token in tokens]
    for _, biases in chunks:
        operands += biases
        specs += [whole(bias.shape) for bias in biases]
    aliases = {}
    if buffer is not None:
        aliases = {len(operands): 0}
        specs.append(pl.BlockSpec(memory_space=pl.ANY))
        operands.append(buffer)
    return pl.pallas_call(
        attend_kernel if len(chunks) == 1 else attend_late_kernel,
        grid_spec=pltpu.PrefetchScalarGridSpec(
            num_scalar_prefetch=1,
            grid=(rows,),
            in_specs=specs,
            out_specs=pl.BlockSpec(out_block, out_index),
        ),
        out_shape=jax.ShapeDtypeStruct(out_shape, BF16),
        input_output_aliases=aliases,
        compiler_params=params(),
        cost_estimate=cost(time * 100),
    )(*operands)


def single_project_kernel(place_ref, single_ref, gain_ref, weight_ref, kv_ref, qg_ref):
    normed = normalize(single_ref[...], gain_ref[...])
    for kind in range(2):
        both = dot_nt(weight_ref[1 + kind], normed).astype(BF16)
        for head in range(2):
            kv_ref[head, kind] = both[SINGLE_HEAD_DIM * head : SINGLE_HEAD_DIM * (head + 1)]
    start = pl.multiple_of(place_ref[0], 16)
    own = normalize(single_ref[pl.ds(start, ROWS)], gain_ref[...])
    q = dot_nt(own, weight_ref[0]) * (LOG2E / math.sqrt(SINGLE_HEAD_DIM))
    g = jax.nn.sigmoid(dot_nt(own, weight_ref[3]))
    for kind, value in enumerate((q, g)):
        turned = jnp.concatenate([value[:, SINGLE_HEAD_DIM:], value[:, :SINGLE_HEAD_DIM]], axis=1)
        qg_ref[kind] = jnp.where(place_ref[1] == 1, turned, value)


def single_project(place, single, gain, weight):
    return pl.pallas_call(
        single_project_kernel,
        grid_spec=pltpu.PrefetchScalarGridSpec(
            num_scalar_prefetch=1,
            grid=(1,),
            in_specs=[
                whole((TOKENS, SINGLE_DIM)),
                whole((1, SINGLE_DIM)),
                whole((4, COLS, SINGLE_DIM)),
            ],
            out_specs=[whole((2, 2, SINGLE_HEAD_DIM, TOKENS)), whole((2, ROWS, COLS))],
        ),
        out_shape=[
            jax.ShapeDtypeStruct((2, 2, SINGLE_HEAD_DIM, TOKENS), BF16),
            jax.ShapeDtypeStruct((2, ROWS, COLS), F32),
        ],
        compiler_params=params(),
        cost_estimate=cost(4),
    )(place, single, gain, weight)


def single_kernel(
    place_ref, early_ref, late_ref, gain_ref, weight_ref, extra_ref, *rest
):
    heads = SINGLE_HEADS
    shared, rep_ref, out_ref, held = rest[:8], rest[8], rest[9], rest[10]
    for core in range(2):
        for slot in range(4):
            held[core, lax.rem(place_ref[1] + slot, 4)] = shared[4 * core + slot][...]
    weight = weight_ref[...].astype(F32)
    line = lax.broadcasted_iota(jnp.int32, weight.shape, 0)
    turned = jnp.where(line % 2 == 0, pltpu.roll(weight, heads - 1, 0), pltpu.roll(weight, 1, 0))
    weight = jnp.where(place_ref[2] == 1, turned, weight).astype(BF16)
    biases = []
    for i in range(MINE):
        tokens = early_ref[:, i] if i < 4 else late_ref[:, 6 * (i - 4) : 6 * (i - 3)]
        normed = normalize(tokens.reshape(TOKENS, CHANNELS), gain_ref[...])
        biases.append(dot_nt(weight, normed).astype(BF16).astype(F32))
    bias = jnp.concatenate(biases, axis=0) * LOG2E

    def piece(core, col, kind, band, third):
        at = 9 * kind + 3 * band + third
        return held[core, at // 7, col, at % 7]

    def matrix(kind):
        rows = []
        for col in range(8):
            for core in range(2):
                for band in range(3):
                    rows.append(
                        jnp.concatenate([piece(core, col, kind, band, third) for third in range(3)], axis=1)
                    )
        return jnp.concatenate(rows, axis=0)

    def vectors(low):
        return jnp.concatenate(
            [extra_ref[col, 0, low : low + MINE, :COLS].astype(F32) for col in range(8)], axis=1
        )

    q = vectors(0)
    g = vectors(8)
    channel = lax.broadcasted_iota(jnp.int32, (heads, SINGLE_DIM), 1)
    low = lax.broadcasted_iota(jnp.int32, (heads, SINGLE_DIM), 0) * SINGLE_HEAD_DIM
    inside = (channel >= low) & (channel < low + SINGLE_HEAD_DIM)
    spread = [
        jnp.where(inside, jnp.broadcast_to(q[i : i + 1], (heads, SINGLE_DIM)), 0.0)
        for i in range(MINE)
    ]
    scores = dot(jnp.concatenate(spread, axis=0).astype(BF16), matrix(0)) + bias
    key = lax.broadcasted_iota(jnp.int32, (1, TOKENS), 1)
    scores = jnp.where(key < place_ref[0], scores, MASKED)
    top = jnp.max(scores, axis=1, keepdims=True)
    exponent = jnp.exp2(scores - top)
    total = jnp.sum(exponent, axis=1, keepdims=True)
    mixed = dot_nt((exponent / total).astype(BF16), matrix(1))
    rows = [
        jnp.sum(jnp.where(inside, mixed[heads * i : heads * (i + 1)], 0.0), axis=0, keepdims=True)
        for i in range(MINE)
    ]
    hidden = (g * jnp.concatenate(rows, axis=0)).astype(BF16)
    result = rep_ref[...].astype(F32) + dot(hidden, matrix(2))
    result = jnp.concatenate([result, jnp.zeros((16 - MINE, SINGLE_DIM), F32)], axis=0)
    out_ref[...] = jnp.zeros(out_ref.shape, BF16)
    for col in range(8):
        out_ref[col, 0, :, :COLS] = result[:, COLS * col : COLS * (col + 1)].astype(BF16)


def single_attend(place, early, late, gain, weight, pair, shared, rep):
    shape = (8, 7, 16, CHANNELS)
    last = lambda *_: (0, 3 * MINE, 0, 0)
    return pl.pallas_call(
        single_kernel,
        grid_spec=pltpu.PrefetchScalarGridSpec(
            num_scalar_prefetch=1,
            grid=(1,),
            in_specs=[
                whole((8, 4, 2, ROWS, CHANNELS)),
                whole((8, 2 * MINE + 1, 16, CHANNELS)),
                whole((1, CHANNELS)),
                whole((SINGLE_HEADS, CHANNELS)),
                pl.BlockSpec((8, 1, 16, CHANNELS), last),
            ]
            + [whole(shape)] * 8
            + [whole((MINE, SINGLE_DIM))],
            scratch_shapes=[pltpu.VMEM((2, 4) + shape, BF16)],
            out_specs=pl.BlockSpec((8, 1, 16, CHANNELS), lambda *_: (0, 2 * MINE, 0, 0)),
        ),
        out_shape=jax.ShapeDtypeStruct((8, 2 * MINE + 1, 16, CHANNELS), BF16),
        input_output_aliases={2: 0},
        compiler_params=params(),
        cost_estimate=cost(700),
    )(place, early, late, gain, weight, pair, *shared, rep)


def exchange(value):
    return lax.all_to_all(value, COL, split_axis=0, concat_axis=0, tiled=True)


Z = ("zl", "zh")


def shift(value, axis, by):
    if axis == Z:
        ring = [0, 2, 1, 3]
        pairs = [(ring[i], ring[(i + by) % 4]) for i in range(4)]
    else:
        size = lax.axis_size(axis)
        pairs = [(i, (i + by) % size) for i in range(size)]
    return lax.ppermute(value, axis, pairs)


def around(value, axis):
    return [value, shift(value, axis, -1), shift(value, axis, 2), shift(value, axis, 1)]


def per_device(
    pair_rep,
    single_rep,
    length,
    pair_gain,
    pair_proj,
    bias_weight,
    pair_out_weight,
    single_gain,
    single_proj,
    bias_norm_gain,
    single_bias_weight,
    single_out_weight,
):
    core = lax.axis_index("core")
    x = lax.axis_index("x")
    row = lax.axis_index(ROW)
    col = lax.axis_index(COL)
    second_core = core == 1
    pair_gain = pair_gain.reshape(1, CHANNELS)

    groups = pair_rep.reshape(8, 6 * MINE, 16, CHANNELS)
    limit = length - col * COLS
    bias = local_bias(limit, pair_rep, pair_gain, bias_weight.T)
    kept = lax.dynamic_index_in_dim(bias, core, 0, False)
    given = lax.dynamic_index_in_dim(bias, 1 - core, 0, False)
    taken = shift(given, "core", 1)
    block = jnp.where(second_core, jnp.stack([taken, kept]), jnp.stack([kept, taken]))
    sides = jnp.stack(around(block, "y"))
    after, sides = lax.optimization_barrier((single_rep, sides))
    kv, qg = single_project(
        jnp.stack([row * ROWS, core]),
        after,
        single_gain.reshape(1, SINGLE_DIM),
        jnp.swapaxes(single_proj, 1, 2),
    )
    pieces = around(sides, Z)
    extra = qg.astype(BF16).reshape(2, 8, MINE, COLS)
    extra = jnp.pad(jnp.swapaxes(extra, 0, 1), ((0, 0), (0, 0), (0, 2), (0, CHANNELS - COLS)))
    shared = jnp.concatenate(
        [
            lax.dynamic_index_in_dim(kv, core, 0, False),
            lax.dynamic_slice_in_dim(single_out_weight, core * SINGLE_HEAD_DIM, SINGLE_HEAD_DIM, 0)[None],
        ],
        axis=0,
    )
    shared = jnp.transpose(shared.reshape(3, 3, 16, 3, CHANNELS), (0, 1, 3, 2, 4)).reshape(27, 16, CHANNELS)
    shared = jnp.pad(shared, ((0, 1), (0, 0), (0, 0)))
    shared = lax.dynamic_slice_in_dim(shared, 7 * x, 7, 0)
    message = jnp.concatenate(
        [
            groups[:, 3 * MINE :],
            extra.reshape(8, 1, 16, CHANNELS),
            jnp.broadcast_to(shared[None], (8, 7, 16, CHANNELS)),
        ],
        axis=1,
    )
    near, pieces = lax.optimization_barrier((groups[:, : 3 * MINE], pieces))
    near = exchange(near)
    message, near = lax.optimization_barrier((message, near))
    far = exchange(message)

    turned = jnp.where(second_core, jnp.roll(pair_proj, 128, axis=2), pair_proj)
    wo = jnp.where(second_core, jnp.roll(pair_out_weight, 128, axis=0), pair_out_weight)
    weights = (pair_gain, turned[0], turned[1].T, turned[2], turned[3])
    held = project(near, *weights, 0, ())

    depth = 2 * lax.axis_index("zh") + lax.axis_index("zl")
    chunks = join(jnp.stack([lax.axis_index("y"), depth]), pieces)
    firsts = [around(chunks[0], "x")]
    chunk, firsts[0][1] = lax.optimization_barrier((chunks[1], firsts[0][1]))
    firsts.append(around(chunk, "x"))
    seconds = [[shift(item, "core", 1) for item in items] for items in firsts]
    shared = far[:, 3 * MINE + 1 :]
    shared, _ = lax.optimization_barrier((shared, firsts[1][1]))
    shared = around(shared, "x")
    swapped = [shift(item, "core", 1) for item in shared]

    held = project(far, *weights, MINE // 2, held)
    kt, v = held[:2]
    tokens = [list(held[2 + chunk :: 2]) for chunk in range(2)]
    biases = [firsts[chunk] + seconds[chunk] for chunk in range(2)]
    parts = [(tokens[chunk], biases[chunk]) for chunk in range(2)]
    x1 = x.reshape(1)
    shape = (8, 4, 2, ROWS, CHANNELS)
    early = attend(
        x1, kt, v, wo, parts[:1], 4, 0, (8, 1, 2, 16, CHANNELS), lambda i, x: (0, i, 0, 2, 0), shape, None, 12
    )
    early = attend(
        x1, kt, v, wo, parts[1:], 4, 0, (8, 1, 2, 32, CHANNELS), lambda i, x: (0, i, 0, 0, 0), shape, early, 22
    )
    early, _ = lax.optimization_barrier((early, shared))
    late = attend(
        x1, kt, v, wo, parts, 2, 4, (8, 6, 16, CHANNELS), lambda i, x: (0, i, 0, 0), (8, 13, 16, CHANNELS), None, 16
    )
    rep = lax.dynamic_slice_in_dim(single_rep, row * ROWS + col * MINE, MINE, 0)
    late = single_attend(
        jnp.concatenate([length, x1, core.reshape(1)]),
        early,
        late,
        bias_norm_gain.reshape(1, CHANNELS),
        single_bias_weight.T,
        far,
        shared + swapped,
        rep,
    )
    early = exchange(early)
    early, late = lax.optimization_barrier((early, late))
    late = exchange(late)
    single_out = late[:, 2 * MINE, :MINE, :COLS].reshape(ROWS, COLS)
    parts = [early.reshape(8, 4, COLS, CHANNELS), late[:, : 2 * MINE].reshape(8, 2, COLS, CHANNELS)]
    return jnp.concatenate(parts, axis=1).reshape(ROWS, COLS, CHANNELS), single_out


def solution(mesh):
    fine = Mesh(mesh.devices.reshape(4, 2, 2, 4, 2), ROW + COL)
    in_specs = (
        P(ROW, COL, None),
        P(),
        P(),
        P(),
        P(),
        P(),
        P(),
        P(),
        P(None, None, COL),
        P(),
        P(),
        P(COL, None),
    )
    out_specs = (P(ROW, COL, None), P(ROW, COL))
    return jax.shard_map(
        per_device, mesh=fine, in_specs=in_specs, out_specs=out_specs, check_vma=False
    )
```

time: 265 us -> 221 us (0.83)
  waiting for transfers between devices: 72.5 us -> 48 us
  starting transfers between devices: 23.7 us -> 42.1 us
  between operations: 14.8 us -> 1.84 us
  blocking collectives: 35.3 us -> 22.8 us
  local copies, waits for them, and re-layouts: 22.2 us -> 13.4 us
  Pallas kernels: 89.6 us -> 86.1 us
    all_to_all x4 -> x3, waiting for transfers between devices: 26.8 us -> 2.77 us  [exchange(): return lax.all_to_all(value, COL, split_axis=0, concat_axis=0, tiled=True)]
    ppermute x8 -> x28, starting transfers between devices: 5.08 us -> 27.2 us  [shift(): return lax.ppermute(value, axis, pairs)]
    all_to_all x1, blocking collectives: 35.3 us -> 22.8 us  [exchange(): return lax.all_to_all(value, COL, split_axis=0, concat_axis=0, tiled=True)]
    pallas_call x6, Pallas kernels: 74.5 us -> 68.8 us  [the longest x3 54.3 us: attend(): pl.pallas_call(attend_kernel if len(chunks) == 1 else attend_late_kernel,...]
    slice x6 -> x4, local copies, waits for them, and re-layouts: 6.56 us -> 1.73 us  [the longest x1 1.63 us: per_device(): near, pieces = lax.optimization_barrier((groups[:, :3 * MINE], pieces))]
    unnamed x13 -> x55, local copies, waits for them, and re-layouts: 1.43 us -> 5.53 us
    all_to_all x4 -> x3, starting transfers between devices: 18.6 us -> 14.9 us  [exchange(): return lax.all_to_all(value, COL, split_axis=0, concat_axis=0, tiled=True)]
    ppermute x8 -> x28, waiting for transfers between devices: 45.7 us -> 45.2 us  [shift(): return lax.ppermute(value, axis, pairs)]
  transfers between devices with their start and end apart: 13 -> 31, of which waited for: 6 -> 10; matrix products, arithmetic and copies ran while one was open for 8% -> 5% of each run, Pallas kernels for 33% -> 36%
where the time goes in v2:
time: 221 us; the launch traced here: 220 us
  Pallas kernels  86.1 us (39%)
  waiting for transfers between devices  48 us (22%)
  starting transfers between devices  42.1 us (19%)
  blocking collectives  22.8 us (10%)
  local copies, waits for them, and re-layouts  13.4 us (6%)
  other arithmetic  6.01 us (3%)
    pallas_call x3, Pallas kernels, attend(): pl.pallas_call(attend_kernel if len(chunks) == 1 else attend_late_kernel,...  54.3 us
    ppermute x28, waiting for transfers between devices, shift(): return lax.ppermute(value, axis, pairs)  45.2 us
    ppermute x28, starting transfers between devices, shift(): return lax.ppermute(value, axis, pairs)  27.2 us
    all_to_all x1, blocking collectives, exchange(): return lax.all_to_all(value, COL, split_axis=0, concat_axis=0, tiled=True)  22.8 us
    all_to_all x3, starting transfers between devices, exchange(): return lax.all_to_all(value, COL, split_axis=0, concat_axis=0, tiled=True)  14.9 us
    pallas_call x2, Pallas kernels, project(): pl.pallas_call(project_kernel, grid=(MINE // 2,), in_specs=[pl.BlockSpec(...  10.8 us
    pallas_call x1, Pallas kernels, single_attend(): pl.pallas_call(single_kernel, grid_spec=pltpu.PrefetchScalarGridSpec(num_...  7.25 us
    pallas_call x1, Pallas kernels, local_bias(): pl.pallas_call(local_bias_kernel, grid_spec=pltpu.PrefetchScalarGridSpec(...  5.91 us
  transfers between devices with their start and end apart: 31, of which 10 were waited for; matrix products, arithmetic and copies ran while one was open for 5% of the time, Pallas kernels for 36%

profile of v2, /device:TPU:0, one launch (start us, length us, event | category | flops | bytes accessed | tf_op | source)
XLA Modules:
  0.0 220.3 jit_solution(16752954144690516595)
XLA Ops:
  1.4 5.9 %shard_map.131 = bf16[2,48,384]{2,1,0:T(8,128)(2,1)} custom-call(s32[1]{0:T(128)S(6)} %sub.10.limit_ref, bf16[48,96,256]{2,1,0:T(8,128)(2,1)} %pair_ref.1, f32[1,256]{1,0:T(1,128)} %bitcast.56, bf16[8,256]{1,0:T(8,128)(2,1)} %bitcast.59), custom_call_target="tpu_custom_call" | custom-call | flops 50000000 | bytes 150000 | tf_op jit(solution)/shard_map/pallas_call | solution.py:79
  7.3 0.8 dynamic-slice_bitcast_fusion
  8.1 1.2 collective-permute-done
  9.4 1.7 collective-permute-start.3
  11.1 2.9 %collective-permute-start.2 = (bf16[2,48,384]{2,1,0:T(8,128)(2,1)S(1)}, bf16[2,48,384]{2,1,0:T(8,128)(2,1)S(1)}, u32[]{:S(2)}, u32[]{:S(2)}) collective-permute-start(bf16[2,48,384]{2,1,0:T(8,128)(2,1)S(1)} %maximum_select_fusion.3), channel_id=1, source_target_pairs={{0,4},{2,6},{4,0},{6,2},{1,5},{3,7},{5,1},{7,3},{8,12},{10,14},{12... | collective-permute-start | bytes 221192 | tf_op jit(solution)/shard_map/ppermute | solution.py:414
  14.0 1.3 collective-permute-start.1
  15.4 2.5 %collective-permute-done.2 = bf16[2,48,384]{2,1,0:T(8,128)(2,1)S(1)} collective-permute-done((bf16[2,48,384]{2,1,0:T(8,128)(2,1)S(1)}, bf16[2,48,384]{2,1,0:T(8,128)(2,1)S(1)}, u32[]{:S(2)}, u32[]{:S(2)}) %collective-permute-start.2) | collective-permute-done | bytes 73760 | tf_op jit(solution)/shard_map/ppermute | solution.py:414
  18.4 4.1 %collective-permute-start.4 = (bf16[4,2,48,384]{3,2,1,0:T(8,128)(2,1)S(1)}, bf16[4,2,48,384]{3,2,1,0:T(8,128)(2,1)S(1)}, u32[]{:S(2)}, u32[]{:S(2)}) collective-permute-start(bf16[4,2,48,384]{3,2,1,0:T(8,128)(2,1)S(1)} %pad_maximum_fusion.2.a_ref), channel_id=1, source_target_pairs={{0,17},{16,0},{1,16},{17,1},{2,19},{18,2},{3,18},{19,3},{4,21},{20... | collective-permute-start | bytes 884744 | tf_op jit(solution)/shard_map/ppermute | solution.py:414
  22.5 1.3 collective-permute-start.6
  23.8 1.6 fusion
  25.4 8.7 %collective-permute-done.4.b_ref = bf16[4,2,48,384]{3,2,1,0:T(8,128)(2,1)S(1)} collective-permute-done((bf16[4,2,48,384]{3,2,1,0:T(8,128)(2,1)S(1)}, bf16[4,2,48,384]{3,2,1,0:T(8,128)(2,1)S(1)}, u32[]{:S(2)}, u32[]{:S(2)}) %collective-permute-start.4) | collective-permute-done | bytes 294944 | tf_op jit(solution)/shard_map/ppermute | solution.py:414
  34.1 3.4 %collective-permute-done.6.d_ref = bf16[4,2,48,384]{3,2,1,0:T(8,128)(2,1)S(1)} collective-permute-done((bf16[4,2,48,384]{3,2,1,0:T(8,128)(2,1)S(1)}, bf16[4,2,48,384]{3,2,1,0:T(8,128)(2,1)S(1)}, u32[]{:S(2)}, u32[]{:S(2)}) %collective-permute-start.6) | collective-permute-done | bytes 294944 | tf_op jit(solution)/shard_map/ppermute | solution.py:414
  37.6 3.6 %all-to-all-start = ((bf16[8,18,16,256]{3,2,1,0:T(8,128)(2,1)}), bf16[8,18,16,256]{3,2,1,0:T(8,128)(2,1)S(1)}, u32[]{:S(2)}, u32[]{:S(2)}) async-start(bf16[8,18,16,256]{3,2,1,0:T(8,128)(2,1)} %get-tuple-element.41), calls=%async_computation | async-start | bytes 2359296 | tf_op jit(solution)/shard_map/all_to_all | solution.py:401
  43.1 4.2 %shard_map.132 = (bf16[2,2,48,768]{3,2,1,0:T(8,128)(2,1)}, f32[2,48,96]{2,1,0:T(8,128)}) custom-call(s32[2]{0:T(128)} %pad_add_fusion.place_ref, bf16[768,768]{1,0:T(8,128)(2,1)} %single_ref, f32[1,768]{1,0:T(1,128)} %reshape.104.gain_ref, bf16[4,96,768]{2,1,0:T(8,128)(2,1)} %bitcast.48), custom_call_target="tpu_custom_call" | custom-call | flops 40000000 | bytes 120000 | tf_op jit(solution)/shard_map/pallas_call | solution.py:286
  47.2 0.9 constant_dynamic-slice_fusion.2
  48.6 3.7 %shard_map.135 = (bf16[4,64,768]{2,1,0:T(8,128)(2,1)}, bf16[4,128,768]{2,1,0:T(8,128)(2,1)}) custom-call(s32[2]{0:T(128)} %pad_add_fusion.1.place_ref, bf16[4,2,48,384]{3,2,1,0:T(8,128)(2,1)} %copy-done.6, bf16[4,2,48,384]{3,2,1,0:T(8,128)(2,1)} %copy-done.9, bf16[4,2,48,384]{3,2,1,0:T(8,128)(2,1)} %copy-done.10, bf16[4,2,48,384]{3,2,1,0:T(8,128)(2,1)} %copy-done.11), custom_call_target="tpu_custom_call" | custom-call | flops 30000000 | bytes 90000 | tf_op jit(solution)/shard_map/pallas_call | solution.py:120
  52.3 2.8 %collective-permute-start.7 = (bf16[4,64,768]{2,1,0:T(8,128)(2,1)}, bf16[4,64,768]{2,1,0:T(8,128)(2,1)}, u32[]{:S(2)}, u32[]{:S(2)}) collective-permute-start(bf16[4,64,768]{2,1,0:T(8,128)(2,1)} %get-tuple-element.62.rest_0_), channel_id=1, source_target_pairs={{0,96},{32,0},{64,32},{96,64},{1,97},{33,1},{65,33},{97,65},{2,98}... | collective-permute-start | bytes 1179656 | tf_op jit(solution)/shard_map/ppermute | solution.py:414
  55.1 1.4 pad_maximum_fusion.1
  56.6 2.8 %all-to-all-done.pair_ref = bf16[8,18,16,256]{3,2,1,0:T(8,128)(2,1)S(1)} async-done(((bf16[8,18,16,256]{3,2,1,0:T(8,128)(2,1)}), bf16[8,18,16,256]{3,2,1,0:T(8,128)(2,1)S(1)}, u32[]{:S(2)}, u32[]{:S(2)}) %all-to-all-start) | async-done | bytes 1179680 | tf_op jit(solution)/shard_map/all_to_all | solution.py:401
  59.3 1.0 copy-done.3
  60.4 4.3 %all-to-all-start.1 = ((bf16[8,26,16,256]{3,2,1,0:T(8,128)(2,1)}), bf16[8,26,16,256]{3,2,1,0:T(8,128)(2,1)S(1)}, u32[]{:S(2)}, u32[]{:S(2)}) async-start(bf16[8,26,16,256]{3,2,1,0:T(8,128)(2,1)} %pad_maximum_fusion.1), calls=%async_computation.1 | async-start | bytes 3407872 | tf_op jit(solution)/shard_map/all_to_all | solution.py:401
  64.7 2.4 %collective-permute-start.15 = (bf16[4,64,768]{2,1,0:T(8,128)(2,1)}, bf16[4,64,768]{2,1,0:T(8,128)(2,1)}, u32[]{:S(2)}, u32[]{:S(2)}) collective-permute-start(bf16[4,64,768]{2,1,0:T(8,128)(2,1)} %get-tuple-element.62.rest_0_), channel_id=1, source_target_pairs={{0,64},{32,96},{64,0},{96,32},{1,65},{33,97},{65,1},{97,33},{2,66}... | collective-permute-start | bytes 1179656 | tf_op jit(solution)/shard_map/ppermute | solution.py:414
  67.1 1.1 collective-permute-start.8
  68.5 1.0 collective-permute-start.16
  69.4 1.3 collective-permute-start.9
  70.7 8.0 %collective-permute-done.15.rest_2_ = bf16[4,64,768]{2,1,0:T(8,128)(2,1)} collective-permute-done((bf16[4,64,768]{2,1,0:T(8,128)(2,1)}, bf16[4,64,768]{2,1,0:T(8,128)(2,1)}, u32[]{:S(2)}, u32[]{:S(2)}) %collective-permute-start.15) | collective-permute-done | bytes 393248 | tf_op jit(solution)/shard_map/ppermute | solution.py:414
  78.7 0.7 collective-permute-start.10
  79.5 0.8 slice_bitcast_fusion
  80.2 6.8 %collective-permute-done.16.rest_3_ = bf16[4,64,768]{2,1,0:T(8,128)(2,1)S(1)} collective-permute-done((bf16[4,64,768]{2,1,0:T(8,128)(2,1)S(1)}, bf16[4,64,768]{2,1,0:T(8,128)(2,1)S(1)}, u32[]{:S(2)}, u32[]{:S(2)}) %collective-permute-start.16) | collective-permute-done | bytes 393248 | tf_op jit(solution)/shard_map/ppermute | solution.py:414
  87.9 7.0 %collective-permute-done.8.rest_1_.rest_9_ = bf16[4,128,768]{2,1,0:T(8,128)(2,1)} collective-permute-done((bf16[4,128,768]{2,1,0:T(8,128)(2,1)}, bf16[4,128,768]{2,1,0:T(8,128)(2,1)}, u32[]{:S(2)}, u32[]{:S(2)}) %collective-permute-start.8) | collective-permute-done | bytes 786464 | tf_op jit(solution)/shard_map/ppermute | solution.py:414
  95.5 0.7 copy.35.wkt_ref
  96.3 1.3 constant_dynamic-slice_fusion.rest_8_
  98.3 5.4 %shard_map.133 = (bf16[6,256,768]{2,1,0:T(8,128)(2,1)}, bf16[6,768,256]{2,1,0:T(8,128)(2,1)}, bf16[6,4,64,256]{3,2,1,0:T(8,128)(2,1)}, bf16[6,4,128,256]{3,2,1,0...) custom-call(bf16[8,18,16,256]{3,2,1,0:T(8,128)(2,1)} %copy-done.3, ...), custom_call_target="tpu_custom_call" | custom-call | flops 50000000 | bytes 150000 | tf_op jit(solution)/shard_map/pallas_call | solution.py:159
  103.7 1.2 copy-done.2
  104.9 5.4 %shard_map.134 = (bf16[6,256,768]{2,1,0:T(8,128)(2,1)}, bf16[6,768,256]{2,1,0:T(8,128)(2,1)}, bf16[6,4,64,256]{3,2,1,0:T(8,128)(2,1)}, bf16[6,4,128,256]{3,2,1,0...) custom-call(bf16[8,26,16,256]{3,2,1,0:T(8,128)(2,1)} %copy-done.2, ...), custom_call_target="tpu_custom_call", output_to_operand_aliasing={{0}: (6, {}), {1}: (7, {}), {2}: (8, {}), {3}: (9, {}), {4}... | custom-call | flops 50000000 | bytes 150000 | tf_op jit(solution)/shard_map/pallas_call | solution.py:159
  110.3 0.8 collective-permute-start.11
  111.6 7.1 %collective-permute-done.10.rest_3_.rest_11_ = bf16[4,128,768]{2,1,0:T(8,128)(2,1)} collective-permute-done((bf16[4,128,768]{2,1,0:T(8,128)(2,1)}, bf16[4,128,768]{2,1,0:T(8,128)(2,1)}, u32[]{:S(2)}, u32[]{:S(2)}) %collective-permute-start.10) | collective-permute-done | bytes 786464 | tf_op jit(solution)/shard_map/ppermute | solution.py:414
  119.3 13.2 %shard_map.136.rest_8_ = bf16[8,4,2,48,256]{4,3,2,1,0:T(8,128)(2,1)} custom-call(s32[1]{0:T(128)} %bitcast.x_ref, bf16[6,256,768]{2,1,0:T(8,128)(2,1)} %get-tuple-element.52.kt_ref, bf16[6,768,256]{2,1,0:T(8,128)(2,1)} %get-tuple-element.53.v_ref, bf16[256,256]{1,0:T(8,128)(2,1)} %maximum_select_fusion.1.wo_ref, ...), custom_call_target="tpu_custom_call" | custom-call | flops 12000000000 | bytes 36000000 | tf_op jit(solution)/shard_map/pallas_call | solution.py:255
  132.5 2.6 %collective-permute-start.22 = (bf16[8,7,16,256]{3,2,1,0:T(8,128)(2,1)S(1)}, bf16[8,7,16,256]{3,2,1,0:T(8,128)(2,1)S(1)}, u32[]{:S(2)}, u32[]{:S(2)}) collective-permute-start(bf16[8,7,16,256]{3,2,1,0:T(8,128)(2,1)S(1)} %slice.62.rest_0_), channel_id=1, source_target_pairs={{0,64},{32,96},{64,0},{96,32},{1,65},{33,97},{65,1},{97,33},{2,66}... | collective-permute-start | bytes 1376264 | tf_op jit(solution)/shard_map/ppermute | solution.py:414
  135.1 0.8 collective-permute-start.23
  136.0 0.8 copy-done.16
  137.1 22.2 %shard_map.137.early_ref = bf16[8,4,2,48,256]{4,3,2,1,0:T(8,128)(2,1)} custom-call(s32[1]{0:T(128)} %bitcast.x_ref, bf16[6,256,768]{2,1,0:T(8,128)(2,1)} %get-tuple-element.52.kt_ref, bf16[6,768,256]{2,1,0:T(8,128)(2,1)} %get-tuple-element.53.v_ref, bf16[256,256]{1,0:T(8,128)(2,1)} %maximum_select_fusion.1.wo_ref, ...), custom_call_target="tpu_custom_call", output_to_operand_aliasing={{}: (15, {})} | custom-call | flops 22000001024 | bytes 66000000 | tf_op jit(solution)/shard_map/pallas_call | solution.py:255
  159.4 0.8 copy-done.19
  160.2 7.0 %all-to-all-start.2 = ((bf16[8,4,2,48,256]{4,3,2,1,0:T(8,128)(2,1)}), bf16[8,4,2,48,256]{4,3,2,1,0:T(8,128)(2,1)S(1)}, u32[]{:S(2)}, u32[]{:S(2)}) async-start(bf16[8,4,2,48,256]{4,3,2,1,0:T(8,128)(2,1)} %shard_map.137.early_ref), calls=%async_computation.2 | async-start | bytes 3145728 | tf_op jit(solution)/shard_map/all_to_all | solution.py:401
  167.8 18.9 %shard_map.138.late_ref = bf16[8,13,16,256]{3,2,1,0:T(8,128)(2,1)} custom-call(s32[1]{0:T(128)} %bitcast.x_ref, bf16[6,256,768]{2,1,0:T(8,128)(2,1)} %get-tuple-element.52.kt_ref, bf16[6,768,256]{2,1,0:T(8,128)(2,1)} %get-tuple-element.53.v_ref, bf16[256,256]{1,0:T(8,128)(2,1)} %maximum_select_fusion.1.wo_ref, ...), custom_call_target="tpu_custom_call" | custom-call | flops 16000000000 | bytes 48000000 | tf_op jit(solution)/shard_map/pallas_call | solution.py:255
  187.9 7.2 %shard_map.139 = bf16[8,13,16,256]{3,2,1,0:T(8,128)(2,1)} custom-call(s32[3]{0:T(128)} %pad_add_fusion.2.place_ref, bf16[8,4,2,48,256]{4,3,2,1,0:T(8,128)(2,1)} %shard_map.137.early_ref, bf16[8,13,16,256]{3,2,1,0:T(8,128)(2,1)} %shard_map.138.late_ref, f32[1,256]{1,0:T(1,128)} %bitcast.61, bf16[16,256]{1,0:T(8,128)(2,1)} %bitcast.60, ...), custom_call_target="tpu_custom_call", output_to_operand_aliasing={{}: (2, {})} | custom-call | flops 7000000000 | bytes 21000000 | tf_op jit(solution)/shard_map/pallas_call | solution.py:376
  195.1 22.8 %all_to_all.20 = bf16[8,13,16,256]{3,2,1,0:T(8,128)(2,1)S(1)} all-to-all(bf16[8,13,16,256]{3,2,1,0:T(8,128)(2,1)} %shard_map.139), channel_id=1, replica_groups=mesh['x'=4,'zl'=2,'core'=2,'y'=4,'zh'=2] {'y','zh'}, dimensions={0} | all-to-all | bytes 1703936 | tf_op jit(solution)/shard_map/all_to_all | solution.py:401
  218.6 1.6 pad_maximum_fusion
  (112 shorter events, 9.4 us)
Async XLA Ops:
  0.6 40.5 %copy-start = (bf16[96,768]{1,0:T(8,128)(2,1)S(1)}, bf16[96,768]{1,0:T(8,128)(2,1)}, u32[]{:S(2)}) copy-start(bf16[96,768]{1,0:T(8,128)(2,1)} %param.23) | copy-start | bytes 442372
  1.3 22.4 %copy-start.1 = (bf16[48,96,256]{2,1,0:T(8,128)(2,1)S(1)}, bf16[48,96,256]{2,1,0:T(8,128)(2,1)}, u32[]{:S(2)}) copy-start(bf16[48,96,256]{2,1,0:T(8,128)(2,1)} %pair_ref.1) | copy-start | bytes 7077892
  8.1 1.3 collective-permute-start
  9.4 6.0 %collective-permute-start.3 = (bf16[2,48,384]{2,1,0:T(8,128)(2,1)S(1)}, bf16[2,48,384]{2,1,0:T(8,128)(2,1)S(1)}, u32[]{:S(2)}, u32[]{:S(2)}) collective-permute-start(bf16[2,48,384]{2,1,0:T(8,128)(2,1)S(1)} %maximum_select_fusion.3), channel_id=1, source_target_pairs={{0,2},{2,4},{4,6},{6,0},{1,3},{3,5},{5,7},{7,1},{8,10},{10,12},{12... | collective-permute-start | bytes 221192 | tf_op jit(solution)/shard_map/ppermute | solution.py:414
  11.1 6.8 %collective-permute-start.2 = (bf16[2,48,384]{2,1,0:T(8,128)(2,1)S(1)}, bf16[2,48,384]{2,1,0:T(8,128)(2,1)S(1)}, u32[]{:S(2)}, u32[]{:S(2)}) collective-permute-start(bf16[2,48,384]{2,1,0:T(8,128)(2,1)S(1)} %maximum_select_fusion.3), channel_id=1, source_target_pairs={{0,4},{2,6},{4,0},{6,2},{1,5},{3,7},{5,1},{7,3},{8,12},{10,14},{12... | collective-permute-start | bytes 221192 | tf_op jit(solution)/shard_map/ppermute | solution.py:414
  14.0 4.4 %collective-permute-start.1 = (bf16[2,48,384]{2,1,0:T(8,128)(2,1)S(1)}, bf16[2,48,384]{2,1,0:T(8,128)(2,1)S(1)}, u32[]{:S(2)}, u32[]{:S(2)}) collective-permute-start(bf16[2,48,384]{2,1,0:T(8,128)(2,1)S(1)} %maximum_select_fusion.3), channel_id=1, source_target_pairs={{0,6},{2,0},{4,2},{6,4},{1,7},{3,1},{5,3},{7,5},{8,14},{10,8},{12,... | collective-permute-start | bytes 221192 | tf_op jit(solution)/shard_map/ppermute | solution.py:414
  18.4 7.0 %copy-start.6 = (bf16[4,2,48,384]{3,2,1,0:T(8,128)(2,1)}, bf16[4,2,48,384]{3,2,1,0:T(8,128)(2,1)S(1)}, u32[]{:S(2)}) copy-start(bf16[4,2,48,384]{3,2,1,0:T(8,128)(2,1)S(1)} %pad_maximum_fusion.2.a_ref) | copy-start | bytes 884740
  18.4 15.7 %collective-permute-start.4 = (bf16[4,2,48,384]{3,2,1,0:T(8,128)(2,1)S(1)}, bf16[4,2,48,384]{3,2,1,0:T(8,128)(2,1)S(1)}, u32[]{:S(2)}, u32[]{:S(2)}) collective-permute-start(bf16[4,2,48,384]{3,2,1,0:T(8,128)(2,1)S(1)} %pad_maximum_fusion.2.a_ref), channel_id=1, source_target_pairs={{0,17},{16,0},{1,16},{17,1},{2,19},{18,2},{3,18},{19,3},{4,21},{20... | collective-permute-start | bytes 884744 | tf_op jit(solution)/shard_map/ppermute | solution.py:414
  22.5 11.6 %collective-permute-start.5 = (bf16[4,2,48,384]{3,2,1,0:T(8,128)(2,1)S(1)}, bf16[4,2,48,384]{3,2,1,0:T(8,128)(2,1)S(1)}, u32[]{:S(2)}, u32[]{:S(2)}) collective-permute-start(bf16[4,2,48,384]{3,2,1,0:T(8,128)(2,1)S(1)} %pad_maximum_fusion.2.a_ref), channel_id=1, source_target_pairs={{0,1},{16,17},{1,0},{17,16},{2,3},{18,19},{3,2},{19,18},{4,5},{20,... | collective-permute-start | bytes 884744 | tf_op jit(solution)/shard_map/ppermute | solution.py:414
  22.5 15.0 %collective-permute-start.6 = (bf16[4,2,48,384]{3,2,1,0:T(8,128)(2,1)S(1)}, bf16[4,2,48,384]{3,2,1,0:T(8,128)(2,1)S(1)}, u32[]{:S(2)}, u32[]{:S(2)}) collective-permute-start(bf16[4,2,48,384]{3,2,1,0:T(8,128)(2,1)S(1)} %pad_maximum_fusion.2.a_ref), channel_id=1, source_target_pairs={{0,16},{16,1},{1,17},{17,0},{2,18},{18,3},{3,19},{19,2},{4,20},{20... | collective-permute-start | bytes 884744 | tf_op jit(solution)/shard_map/ppermute | solution.py:414
  25.4 15.8 %copy-start.13 = (f32[768]{0:T(1024)S(1)}, f32[768]{0:T(1024)}, u32[]{:S(2)}) copy-start(f32[768]{0:T(1024)} %param.19) | copy-start | bytes 9220
  34.1 13.1 %copy-start.9 = (bf16[4,2,48,384]{3,2,1,0:T(8,128)(2,1)}, bf16[4,2,48,384]{3,2,1,0:T(8,128)(2,1)S(1)}, u32[]{:S(2)}) copy-start(bf16[4,2,48,384]{3,2,1,0:T(8,128)(2,1)S(1)} %collective-permute-done.4.b_ref) | copy-start | bytes 884740
  34.1 13.1 %copy-start.10 = (bf16[4,2,48,384]{3,2,1,0:T(8,128)(2,1)}, bf16[4,2,48,384]{3,2,1,0:T(8,128)(2,1)S(1)}, u32[]{:S(2)}) copy-start(bf16[4,2,48,384]{3,2,1,0:T(8,128)(2,1)S(1)} %collective-permute-done.5.c_ref) | copy-start | bytes 884740
  37.5 9.7 %copy-start.11 = (bf16[4,2,48,384]{3,2,1,0:T(8,128)(2,1)}, bf16[4,2,48,384]{3,2,1,0:T(8,128)(2,1)S(1)}, u32[]{:S(2)}) copy-start(bf16[4,2,48,384]{3,2,1,0:T(8,128)(2,1)S(1)} %collective-permute-done.6.d_ref) | copy-start | bytes 884740
  37.6 21.8 %all-to-all-start = ((bf16[8,18,16,256]{3,2,1,0:T(8,128)(2,1)}), bf16[8,18,16,256]{3,2,1,0:T(8,128)(2,1)S(1)}, u32[]{:S(2)}, u32[]{:S(2)}) async-start(bf16[8,18,16,256]{3,2,1,0:T(8,128)(2,1)} %get-tuple-element.41), calls=%async_computation | async-start | bytes 2359296 | tf_op jit(solution)/shard_map/all_to_all | solution.py:401
  47.2 1.3 copy-start.12
  48.2 6.9 %copy-start.4 = (bf16[8,18,16,256]{3,2,1,0:T(8,128)(2,1)S(1)}, bf16[8,18,16,256]{3,2,1,0:T(8,128)(2,1)}, u32[]{:S(2)}) copy-start(bf16[8,18,16,256]{3,2,1,0:T(8,128)(2,1)} %get-tuple-element.73) | copy-start | bytes 3538948
  52.3 14.8 %collective-permute-start.7 = (bf16[4,64,768]{2,1,0:T(8,128)(2,1)}, bf16[4,64,768]{2,1,0:T(8,128)(2,1)}, u32[]{:S(2)}, u32[]{:S(2)}) collective-permute-start(bf16[4,64,768]{2,1,0:T(8,128)(2,1)} %get-tuple-element.62.rest_0_), channel_id=1, source_target_pairs={{0,96},{32,0},{64,32},{96,64},{1,97},{33,1},{65,33},{97,65},{2,98}... | collective-permute-start | bytes 1179656 | tf_op jit(solution)/shard_map/ppermute | solution.py:414
  56.5 11.7 %copy-start.5 = (bf16[4,256,256]{2,1,0:T(8,128)(2,1)S(1)}, bf16[4,256,256]{2,1,0:T(8,128)(2,1)}, u32[]{:S(2)}) copy-start(bf16[4,256,256]{2,1,0:T(8,128)(2,1)} %param.16) | copy-start | bytes 1572868
  60.4 43.3 %all-to-all-start.1 = ((bf16[8,26,16,256]{3,2,1,0:T(8,128)(2,1)}), bf16[8,26,16,256]{3,2,1,0:T(8,128)(2,1)S(1)}, u32[]{:S(2)}, u32[]{:S(2)}) async-start(bf16[8,26,16,256]{3,2,1,0:T(8,128)(2,1)} %pad_maximum_fusion.1), calls=%async_computation.1 | async-start | bytes 3407872 | tf_op jit(solution)/shard_map/all_to_all | solution.py:401
  64.7 3.8 %copy-start.24 = (bf16[4,64,768]{2,1,0:T(8,128)(2,1)S(1)}, bf16[4,64,768]{2,1,0:T(8,128)(2,1)}, u32[]{:S(2)}) copy-start(bf16[4,64,768]{2,1,0:T(8,128)(2,1)} %get-tuple-element.62.rest_0_) | copy-start | bytes 1179652
  64.7 14.8 %copy-start.7 = (bf16[256,256]{1,0:T(8,128)(2,1)S(1)}, bf16[256,256]{1,0:T(8,128)(2,1)}, u32[]{:S(2)}) copy-start(bf16[256,256]{1,0:T(8,128)(2,1)} %param.18) | copy-start | bytes 393220
  64.7 14.0 %collective-permute-start.15 = (bf16[4,64,768]{2,1,0:T(8,128)(2,1)}, bf16[4,64,768]{2,1,0:T(8,128)(2,1)}, u32[]{:S(2)}, u32[]{:S(2)}) collective-permute-start(bf16[4,64,768]{2,1,0:T(8,128)(2,1)} %get-tuple-element.62.rest_0_), channel_id=1, source_target_pairs={{0,64},{32,96},{64,0},{96,32},{1,65},{33,97},{65,1},{97,33},{2,66}... | collective-permute-start | bytes 1179656 | tf_op jit(solution)/shard_map/ppermute | solution.py:414
  67.1 27.8 %collective-permute-start.8 = (bf16[4,128,768]{2,1,0:T(8,128)(2,1)}, bf16[4,128,768]{2,1,0:T(8,128)(2,1)}, u32[]{:S(2)}, u32[]{:S(2)}) collective-permute-start(bf16[4,128,768]{2,1,0:T(8,128)(2,1)} %get-tuple-element.63.rest_0_.rest_8_), channel_id=1, source_target_pairs={{0,96},{32,0},{64,32},{96,64},{1,97},{33,1},{65,33},{97,65},{2,98}... | collective-permute-start | bytes 2359304 | tf_op jit(solution)/shard_map/ppermute | solution.py:414
  68.5 18.6 %collective-permute-start.16 = (bf16[4,64,768]{2,1,0:T(8,128)(2,1)S(1)}, bf16[4,64,768]{2,1,0:T(8,128)(2,1)S(1)}, u32[]{:S(2)}, u32[]{:S(2)}) collective-permute-start(bf16[4,64,768]{2,1,0:T(8,128)(2,1)S(1)} %copy-done.24), channel_id=1, source_target_pairs={{0,32},{32,64},{64,96},{96,0},{1,33},{33,65},{65,97},{97,1},{2,34}... | collective-permute-start | bytes 1179656 | tf_op jit(solution)/shard_map/ppermute | solution.py:414
  69.4 17.7 %collective-permute-start.17 = (bf16[4,64,768]{2,1,0:T(8,128)(2,1)S(1)}, bf16[4,64,768]{2,1,0:T(8,128)(2,1)S(1)}, u32[]{:S(2)}, u32[]{:S(2)}) collective-permute-start(bf16[4,64,768]{2,1,0:T(8,128)(2,1)S(1)} %copy-done.24), channel_id=1, source_target_pairs={{0,8},{8,0},{1,9},{9,1},{2,10},{10,2},{3,11},{11,3},{4,12},{12,4},... | collective-permute-start | bytes 1179656 | tf_op jit(solution)/shard_map/ppermute | solution.py:414
  69.4 41.8 %collective-permute-start.9 = (bf16[4,128,768]{2,1,0:T(8,128)(2,1)}, bf16[4,128,768]{2,1,0:T(8,128)(2,1)}, u32[]{:S(2)}, u32[]{:S(2)}) collective-permute-start(bf16[4,128,768]{2,1,0:T(8,128)(2,1)} %get-tuple-element.63.rest_0_.rest_8_), channel_id=1, source_target_pairs={{0,64},{32,96},{64,0},{96,32},{1,65},{33,97},{65,1},{97,33},{2,66}... | collective-permute-start | bytes 2359304 | tf_op jit(solution)/shard_map/ppermute | solution.py:414
  78.7 39.9 %collective-permute-start.10 = (bf16[4,128,768]{2,1,0:T(8,128)(2,1)}, bf16[4,128,768]{2,1,0:T(8,128)(2,1)}, u32[]{:S(2)}, u32[]{:S(2)}) collective-permute-start(bf16[4,128,768]{2,1,0:T(8,128)(2,1)} %get-tuple-element.63.rest_0_.rest_8_), channel_id=1, source_target_pairs={{0,32},{32,64},{64,96},{96,0},{1,33},{33,65},{65,97},{97,1},{2,34}... | collective-permute-start | bytes 2359304 | tf_op jit(solution)/shard_map/ppermute | solution.py:414
  87.1 16.6 %copy-start.25 = (bf16[4,64,768]{2,1,0:T(8,128)(2,1)}, bf16[4,64,768]{2,1,0:T(8,128)(2,1)S(1)}, u32[]{:S(2)}) copy-start(bf16[4,64,768]{2,1,0:T(8,128)(2,1)S(1)} %collective-permute-done.16.rest_3_) | copy-start | bytes 1179652
  87.1 23.2 %collective-permute-start.18 = (bf16[4,64,768]{2,1,0:T(8,128)(2,1)}, bf16[4,64,768]{2,1,0:T(8,128)(2,1)}, u32[]{:S(2)}, u32[]{:S(2)}) collective-permute-start(bf16[4,64,768]{2,1,0:T(8,128)(2,1)} %collective-permute-done.7.rest_1_), channel_id=1, source_target_pairs={{0,8},{8,0},{1,9},{9,1},{2,10},{10,2},{3,11},{11,3},{4,12},{12,4},... | collective-permute-start | bytes 1179656 | tf_op jit(solution)/shard_map/ppermute | solution.py:414
  87.1 24.0 %collective-permute-start.19 = (bf16[4,64,768]{2,1,0:T(8,128)(2,1)}, bf16[4,64,768]{2,1,0:T(8,128)(2,1)}, u32[]{:S(2)}, u32[]{:S(2)}) collective-permute-start(bf16[4,64,768]{2,1,0:T(8,128)(2,1)} %collective-permute-done.15.rest_2_), channel_id=1, source_target_pairs={{0,8},{8,0},{1,9},{9,1},{2,10},{10,2},{3,11},{11,3},{4,12},{12,4},... | collective-permute-start | bytes 1179656 | tf_op jit(solution)/shard_map/ppermute | solution.py:414
  94.9 23.8 %collective-permute-start.20 = (bf16[4,64,768]{2,1,0:T(8,128)(2,1)S(1)}, bf16[4,64,768]{2,1,0:T(8,128)(2,1)}, u32[]{:S(2)}, u32[]{:S(2)}) collective-permute-start(bf16[4,64,768]{2,1,0:T(8,128)(2,1)S(1)} %collective-permute-done.16.rest_3_), channel_id=1, source_target_pairs={{0,8},{8,0},{1,9},{9,1},{2,10},{10,2},{3,11},{11,3},{4,12},{12,4},... | collective-permute-start | bytes 1179656 | tf_op jit(solution)/shard_map/ppermute | solution.py:414
  103.7 32.2 %copy-start.8 = (bf16[8,7,16,256]{3,2,1,0:T(8,128)(2,1)}, bf16[8,7,16,256]{3,2,1,0:T(8,128)(2,1)S(1)}, u32[]{:S(2)}) copy-start(bf16[8,7,16,256]{3,2,1,0:T(8,128)(2,1)S(1)} %slice.62.rest_0_) | copy-start | bytes 1376260
  110.3 22.2 %collective-permute-start.11 = (bf16[4,128,768]{2,1,0:T(8,128)(2,1)}, bf16[4,128,768]{2,1,0:T(8,128)(2,1)S(1)}, u32[]{:S(2)}, u32[]{:S(2)}) collective-permute-start(bf16[4,128,768]{2,1,0:T(8,128)(2,1)} %get-tuple-element.63.rest_0_.rest_8_), channel_id=1, source_target_pairs={{0,8},{8,0},{1,9},{9,1},{2,10},{10,2},{3,11},{11,3},{4,12},{12,4},... | collective-permute-start | bytes 2359304 | tf_op jit(solution)/shard_map/ppermute | solution.py:414
  111.1 24.0 %collective-permute-start.12 = (bf16[4,128,768]{2,1,0:T(8,128)(2,1)}, bf16[4,128,768]{2,1,0:T(8,128)(2,1)S(1)}, u32[]{:S(2)}, u32[]{:S(2)}) collective-permute-start(bf16[4,128,768]{2,1,0:T(8,128)(2,1)} %collective-permute-done.8.rest_1_.rest_9_), channel_id=1, source_target_pairs={{0,8},{8,0},{1,9},{9,1},{2,10},{10,2},{3,11},{11,3},{4,12},{12,4},... | collective-permute-start | bytes 2359304 | tf_op jit(solution)/shard_map/ppermute | solution.py:414
  111.2 24.7 %collective-permute-start.13 = (bf16[4,128,768]{2,1,0:T(8,128)(2,1)}, bf16[4,128,768]{2,1,0:T(8,128)(2,1)S(1)}, u32[]{:S(2)}, u32[]{:S(2)}) collective-permute-start(bf16[4,128,768]{2,1,0:T(8,128)(2,1)} %collective-permute-done.9.rest_2_.rest_10_), channel_id=1, source_target_pairs={{0,8},{8,0},{1,9},{9,1},{2,10},{10,2},{3,11},{11,3},{4,12},{12,4},... | collective-permute-start | bytes 2359304 | tf_op jit(solution)/shard_map/ppermute | solution.py:414
  118.7 17.3 %collective-permute-start.14 = (bf16[4,128,768]{2,1,0:T(8,128)(2,1)}, bf16[4,128,768]{2,1,0:T(8,128)(2,1)S(1)}, u32[]{:S(2)}, u32[]{:S(2)}) collective-permute-start(bf16[4,128,768]{2,1,0:T(8,128)(2,1)} %collective-permute-done.10.rest_3_.rest_11_), channel_id=1, source_target_pairs={{0,8},{8,0},{1,9},{9,1},{2,10},{10,2},{3,11},{11,3},{4,12},{12,4},... | collective-permute-start | bytes 2359304 | tf_op jit(solution)/shard_map/ppermute | solution.py:414
  118.7 40.6 %collective-permute-start.21 = (bf16[8,7,16,256]{3,2,1,0:T(8,128)(2,1)S(1)}, bf16[8,7,16,256]{3,2,1,0:T(8,128)(2,1)S(1)}, u32[]{:S(2)}, u32[]{:S(2)}) collective-permute-start(bf16[8,7,16,256]{3,2,1,0:T(8,128)(2,1)S(1)} %slice.62.rest_0_), channel_id=1, source_target_pairs={{0,96},{32,0},{64,32},{96,64},{1,97},{33,1},{65,33},{97,65},{2,98}... | collective-permute-start | bytes 1376264 | tf_op jit(solution)/shard_map/ppermute | solution.py:414
  132.5 3.5 %copy-start.14 = (bf16[4,128,768]{2,1,0:T(8,128)(2,1)}, bf16[4,128,768]{2,1,0:T(8,128)(2,1)S(1)}, u32[]{:S(2)}) copy-start(bf16[4,128,768]{2,1,0:T(8,128)(2,1)S(1)} %collective-permute-done.11.rest_4_.rest_12_) | copy-start | bytes 2359300
  132.5 26.8 %collective-permute-start.22 = (bf16[8,7,16,256]{3,2,1,0:T(8,128)(2,1)S(1)}, bf16[8,7,16,256]{3,2,1,0:T(8,128)(2,1)S(1)}, u32[]{:S(2)}, u32[]{:S(2)}) collective-permute-start(bf16[8,7,16,256]{3,2,1,0:T(8,128)(2,1)S(1)} %slice.62.rest_0_), channel_id=1, source_target_pairs={{0,64},{32,96},{64,0},{96,32},{1,65},{33,97},{65,1},{97,33},{2,66}... | collective-permute-start | bytes 1376264 | tf_op jit(solution)/shard_map/ppermute | solution.py:414
  135.1 25.1 %collective-permute-start.23 = (bf16[8,7,16,256]{3,2,1,0:T(8,128)(2,1)S(1)}, bf16[8,7,16,256]{3,2,1,0:T(8,128)(2,1)}, u32[]{:S(2)}, u32[]{:S(2)}) collective-permute-start(bf16[8,7,16,256]{3,2,1,0:T(8,128)(2,1)S(1)} %slice.62.rest_0_), channel_id=1, source_target_pairs={{0,32},{32,64},{64,96},{96,0},{1,33},{33,65},{65,97},{97,1},{2,34}... | collective-permute-start | bytes 1376264 | tf_op jit(solution)/shard_map/ppermute | solution.py:414
  135.9 50.8 %collective-permute-start.24 = (bf16[8,7,16,256]{3,2,1,0:T(8,128)(2,1)S(1)}, bf16[8,7,16,256]{3,2,1,0:T(8,128)(2,1)}, u32[]{:S(2)}, u32[]{:S(2)}) collective-permute-start(bf16[8,7,16,256]{3,2,1,0:T(8,128)(2,1)S(1)} %slice.62.rest_0_), channel_id=1, source_target_pairs={{0,8},{8,0},{1,9},{9,1},{2,10},{10,2},{3,11},{11,3},{4,12},{12,4},... | collective-permute-start | bytes 1376264 | tf_op jit(solution)/shard_map/ppermute | solution.py:414
  159.3 7.8 %copy-start.18 = (bf16[8,7,16,256]{3,2,1,0:T(8,128)(2,1)}, bf16[8,7,16,256]{3,2,1,0:T(8,128)(2,1)S(1)}, u32[]{:S(2)}) copy-start(bf16[8,7,16,256]{3,2,1,0:T(8,128)(2,1)S(1)} %collective-permute-done.21.rest_1_) | copy-start | bytes 1376260
  160.2 7.1 %copy-start.20 = (bf16[8,7,16,256]{3,2,1,0:T(8,128)(2,1)S(1)}, bf16[8,7,16,256]{3,2,1,0:T(8,128)(2,1)}, u32[]{:S(2)}) copy-start(bf16[8,7,16,256]{3,2,1,0:T(8,128)(2,1)} %copy-done.19) | copy-start | bytes 1376260
  160.2 34.9 %all-to-all-start.2 = ((bf16[8,4,2,48,256]{4,3,2,1,0:T(8,128)(2,1)}), bf16[8,4,2,48,256]{4,3,2,1,0:T(8,128)(2,1)S(1)}, u32[]{:S(2)}, u32[]{:S(2)}) async-start(bf16[8,4,2,48,256]{4,3,2,1,0:T(8,128)(2,1)} %shard_map.137.early_ref), calls=%async_computation.2 | async-start | bytes 3145728 | tf_op jit(solution)/shard_map/all_to_all | solution.py:401
  167.2 19.6 %collective-permute-start.25 = (bf16[8,7,16,256]{3,2,1,0:T(8,128)(2,1)S(1)}, bf16[8,7,16,256]{3,2,1,0:T(8,128)(2,1)S(1)}, u32[]{:S(2)}, u32[]{:S(2)}) collective-permute-start(bf16[8,7,16,256]{3,2,1,0:T(8,128)(2,1)S(1)} %collective-permute-done.21.rest_1_), channel_id=1, source_target_pairs={{0,8},{8,0},{1,9},{9,1},{2,10},{10,2},{3,11},{11,3},{4,12},{12,4},... | collective-permute-start | bytes 1376264 | tf_op jit(solution)/shard_map/ppermute | solution.py:414
  167.3 19.5 %collective-permute-start.26 = (bf16[8,7,16,256]{3,2,1,0:T(8,128)(2,1)S(1)}, bf16[8,7,16,256]{3,2,1,0:T(8,128)(2,1)S(1)}, u32[]{:S(2)}, u32[]{:S(2)}) collective-permute-start(bf16[8,7,16,256]{3,2,1,0:T(8,128)(2,1)S(1)} %copy-done.20), channel_id=1, source_target_pairs={{0,8},{8,0},{1,9},{9,1},{2,10},{10,2},{3,11},{11,3},{4,12},{12,4},... | collective-permute-start | bytes 1376264 | tf_op jit(solution)/shard_map/ppermute | solution.py:414
  167.7 19.1 %collective-permute-start.27 = (bf16[8,7,16,256]{3,2,1,0:T(8,128)(2,1)}, bf16[8,7,16,256]{3,2,1,0:T(8,128)(2,1)S(1)}, u32[]{:S(2)}, u32[]{:S(2)}) collective-permute-start(bf16[8,7,16,256]{3,2,1,0:T(8,128)(2,1)} %collective-permute-done.23.rest_3_), channel_id=1, source_target_pairs={{0,8},{8,0},{1,9},{9,1},{2,10},{10,2},{3,11},{11,3},{4,12},{12,4},... | collective-permute-start | bytes 1376264 | tf_op jit(solution)/shard_map/ppermute | solution.py:414
  (10 other events, 9.5 us)

commit v3 on v2

--- a/solution.py
+++ b/solution.py
@@ -95,7 +95,7 @@
     )(limit, pair, gain, weight)
 
 
-def join_kernel(place_ref, a_ref, b_ref, c_ref, d_ref, o0_ref, o1_ref, held):
+def join_kernel(place_ref, a_ref, b_ref, c_ref, d_ref, out_ref, held):
     y = place_ref[0]
     z = place_ref[1]
     for slot, ref in enumerate((a_ref, b_ref, c_ref, d_ref)):
@@ -109,56 +109,49 @@
                 blocks.append(held[depth, side, core])
             for head in range(4):
                 line = jnp.concatenate([b[:, COLS * head : COLS * (head + 1)] for b in blocks], axis=1)
-                at = 2 * low + core
-                o0_ref[head, 16 * at : 16 * (at + 1)] = line[32:]
-                o1_ref[head, 32 * at : 32 * (at + 1)] = line[:32]
+                at = ROWS * (2 * low + core)
+                out_ref[head, at : at + ROWS] = line
 
 
 def join(place, pieces):
     shape = (4, 2, ROWS, 4 * COLS)
-    outs = [(4, 4 * rows, TOKENS) for rows in (16, 32)]
+    out = (4, 4 * ROWS, TOKENS)
     return pl.pallas_call(
         join_kernel,
         grid_spec=pltpu.PrefetchScalarGridSpec(
             num_scalar_prefetch=1,
             grid=(1,),
             in_specs=[whole(shape)] * 4,
-            out_specs=[whole(out) for out in outs],
+            out_specs=whole(out),
             scratch_shapes=[pltpu.VMEM((4,) + shape, BF16)],
         ),
-        out_shape=[jax.ShapeDtypeStruct(out, BF16) for out in outs],
+        out_shape=jax.ShapeDtypeStruct(out, BF16),
         compiler_params=params(),
         cost_estimate=cost(3),
     )(place, *pieces)
 
 
-def project_kernel(pair_ref, gain_ref, wq_ref, wkt_ref, wv_ref, wg_ref, *rest):
-    kt_ref, v_ref, q0_ref, q1_ref, g0_ref, g1_ref, old0_ref, old1_ref = rest[-8:]
-    old = pair_ref[...].reshape(TOKENS, CHANNELS)
-    normed = normalize(old, gain_ref[...])
+def project_kernel(pair_ref, gain_ref, wq_ref, wkt_ref, wv_ref, wg_ref, kt_ref, v_ref, q_ref, g_ref):
+    normed = normalize(pair_ref[...].reshape(TOKENS, CHANNELS), gain_ref[...])
     q = (dot(normed, wq_ref[...]) * (LOG2E / math.sqrt(HEAD_DIM))).astype(BF16)
     kt_ref[0] = dot_nt(wkt_ref[...], normed).astype(BF16)
     v_ref[0] = dot(normed, wv_ref[...]).astype(BF16)
     g = jax.nn.sigmoid(dot(normed, wg_ref[...])).astype(BF16)
-    for value, ref0, ref1 in ((q, q0_ref, q1_ref), (g, g0_ref, g1_ref), (old, old0_ref, old1_ref)):
-        value = value.reshape(16, ROWS, CHANNELS)
-        ref0[0] = value[:, 32:].reshape(4, 64, CHANNELS)
-        ref1[0] = value[:, :32].reshape(4, 128, CHANNELS)
-
-
-def project(pair, gain, wq, wkt, wv, wg, start, buffers):
+    q_ref[0] = q.reshape(4, 4 * ROWS, CHANNELS)
+    g_ref[0] = g.reshape(4, 4 * ROWS, CHANNELS)
+
+
+def project(pair, gain, wq, wkt, wv, wg):
     square = whole((CHANNELS, CHANNELS))
-    blocks = [(CHANNELS, TOKENS), (TOKENS, CHANNELS)] + [(4, 64, CHANNELS), (4, 128, CHANNELS)] * 3
-    operands = [pair, gain, wq, wkt, wv, wg]
-    aliases = {len(operands) + n: n for n in range(len(buffers))}
+    blocks = [(CHANNELS, TOKENS), (TOKENS, CHANNELS)] + [(4, 4 * ROWS, CHANNELS)] * 2
 
     def spec(block):
         zeros = (0,) * len(block)
-        return pl.BlockSpec((1,) + block, lambda i: (start + i,) + zeros)
+        return pl.BlockSpec((1,) + block, lambda i: (i,) + zeros)
 
     return pl.pallas_call(
         project_kernel,
-        grid=(MINE // 2,),
+        grid=(MINE,),
         in_specs=[
             pl.BlockSpec((8, 6, 16, CHANNELS), lambda i: (0, i, 0, 0)),
             whole((1, CHANNELS)),
@@ -166,17 +159,20 @@
             square,
             square,
             square,
-        ]
-        + [pl.BlockSpec(memory_space=pl.ANY)] * len(buffers),
+        ],
         out_specs=[spec(block) for block in blocks],
         out_shape=[jax.ShapeDtypeStruct((MINE,) + block, BF16) for block in blocks],
-        input_output_aliases=aliases,
         compiler_params=params(),
         cost_estimate=cost(5),
-    )(*operands, *buffers)
-
-
-def attend_chunk(order, span, q_ref, g_ref, old_ref, firsts, seconds, kt, v, wo):
+    )(pair, gain, wq, wkt, wv, wg)
+
+
+def attend_kernel(x_ref, kt_ref, v_ref, q_ref, g_ref, pair_ref, wo_ref, *rest):
+    firsts, seconds, out_ref = rest[:5], rest[5:10], rest[10]
+    order = [lax.rem(x_ref[0] + step, 4) for step in range(4)]
+    span = 4 * ROWS
+    kt = kt_ref[0]
+    v = v_ref[0]
     q = jnp.concatenate([q_ref[0, at] for at in order], axis=0)
     ones = jnp.ones((TOKENS, 128), BF16)
     lane = lax.broadcasted_iota(jnp.int32, (1, CHANNELS), 1)
@@ -184,11 +180,13 @@
     halves = []
     for half, refs in enumerate((firsts, seconds)):
         values = jnp.concatenate([v[:, 128 * half : 128 * half + 128], ones], axis=1)
-        total = jnp.zeros((4 * span, 128), F32)
+        total = jnp.zeros((TOKENS, 128), F32)
         for head in range(4):
             low = HEAD_DIM * (4 * half + head)
             own = jnp.where((lane >= low) & (lane < low + HEAD_DIM), q, jnp.zeros_like(q))
-            bias = jnp.concatenate([ref[head] for ref in refs], axis=0)
+            low_heads, high_heads = refs[2], refs[3]
+            far = low_heads[head] if head < 2 else high_heads[head - 2]
+            bias = jnp.concatenate([refs[0][head], refs[1][head], far, refs[4][head]], axis=0)
             scores = dot(own, kt) + bias.astype(F32)
             top = jnp.max(scores, axis=1, keepdims=True)
             weights = jnp.exp2(scores - top).astype(BF16)
@@ -199,72 +197,39 @@
         halves.append(total)
     attended = jnp.concatenate(halves, axis=1)
     g = jnp.concatenate([g_ref[0, at] for at in order], axis=0)
-    update = dot((g.astype(F32) * attended).astype(BF16), wo)
-    return [
-        (old_ref[0, at].astype(F32) + update[span * step : span * (step + 1)]).astype(BF16)
-        for step, at in enumerate(order)
-    ]
-
-
-def attend_kernel(x_ref, kt_ref, v_ref, wo_ref, q_ref, g_ref, old_ref, *rest):
-    out_ref = rest[-1]
-    order = [lax.rem(x_ref[0] + step, 4) for step in range(4)]
-    span = q_ref.shape[2]
-    parts = attend_chunk(
-        order, span, q_ref, g_ref, old_ref, rest[:4], rest[4:8], kt_ref[0], v_ref[0], wo_ref[...]
-    )
-    for at, part in zip(order, parts):
-        out_ref[pl.ds(2 * at, 2), 0] = part.reshape(2, 2, span // 4, CHANNELS)
-
-
-def attend_late_kernel(x_ref, kt_ref, v_ref, wo_ref, q0_ref, g0_ref, old0_ref, q1_ref, g1_ref, old1_ref, *rest):
-    out_ref = rest[-1]
-    order = [lax.rem(x_ref[0] + step, 4) for step in range(4)]
-    chunks = ((q0_ref, g0_ref, old0_ref, rest[:8]), (q1_ref, g1_ref, old1_ref, rest[8:16]))
-    for chunk, (q_ref, g_ref, old_ref, bias) in enumerate(chunks):
-        span = q_ref.shape[2]
-        parts = attend_chunk(
-            order, span, q_ref, g_ref, old_ref, bias[:4], bias[4:], kt_ref[0], v_ref[0], wo_ref[...]
-        )
-        count = chunk + 1
-        for at, part in zip(order, parts):
-            part = part.reshape(2, 2, count, 16, CHANNELS)
-            for core in range(2):
-                first = 3 * core + (2 if chunk == 0 else 0)
-                out_ref[pl.ds(2 * at, 2), first : first + count] = part[:, core]
-
-
-def attend(x, kt, v, wo, chunks, rows, start, out_block, out_index, out_shape, buffer, time):
+    update = dot((g.astype(F32) * attended).astype(BF16), wo_ref[...])
+    for step, at in enumerate(order):
+        old = pair_ref[pl.ds(2 * at, 2)].reshape(span, CHANNELS).astype(F32)
+        new = (old + update[span * step : span * (step + 1)]).astype(BF16)
+        out_ref[pl.ds(2 * at, 2)] = new.reshape(2, 6, 16, CHANNELS)
+
+
+def attend(x, kt, v, q, g, pair, wo, biases, rows, start, groups, time):
     def spec(shape):
         zeros = (0,) * len(shape)
         return pl.BlockSpec((1,) + shape, lambda i, x: (start + i,) + zeros)
 
-    operands = [x, kt, v, wo]
-    specs = [spec((CHANNELS, TOKENS)), spec((TOKENS, CHANNELS)), whole((CHANNELS, CHANNELS))]
-    for tokens, _ in chunks:
-        operands += tokens
-        specs += [spec(token.shape[1:]) for token in tokens]
-    for _, biases in chunks:
-        operands += biases
-        specs += [whole(bias.shape) for bias in biases]
-    aliases = {}
-    if buffer is not None:
-        aliases = {len(operands): 0}
-        specs.append(pl.BlockSpec(memory_space=pl.ANY))
-        operands.append(buffer)
+    parts = spec((4, 4 * ROWS, CHANNELS))
     return pl.pallas_call(
-        attend_kernel if len(chunks) == 1 else attend_late_kernel,
+        attend_kernel,
         grid_spec=pltpu.PrefetchScalarGridSpec(
             num_scalar_prefetch=1,
             grid=(rows,),
-            in_specs=specs,
-            out_specs=pl.BlockSpec(out_block, out_index),
+            in_specs=[
+                spec((CHANNELS, TOKENS)),
+                spec((TOKENS, CHANNELS)),
+                parts,
+                parts,
+                pl.BlockSpec((8, 6, 16, CHANNELS), lambda i, x: (0, start + i, 0, 0)),
+                whole((CHANNELS, CHANNELS)),
+            ]
+            + [whole(bias.shape) for bias in biases],
+            out_specs=pl.BlockSpec((8, 6, 16, CHANNELS), lambda i, x: (0, i, 0, 0)),
         ),
-        out_shape=jax.ShapeDtypeStruct(out_shape, BF16),
-        input_output_aliases=aliases,
+        out_shape=jax.ShapeDtypeStruct((8, groups, 16, CHANNELS), BF16),
         compiler_params=params(),
         cost_estimate=cost(time * 100),
-    )(*operands)
+    )(x, kt, v, q, g, pair, wo, *biases)
 
 
 def single_project_kernel(place_ref, single_ref, gain_ref, weight_ref, kv_ref, qg_ref):
@@ -318,7 +283,7 @@
     weight = jnp.where(place_ref[2] == 1, turned, weight).astype(BF16)
     biases = []
     for i in range(MINE):
-        tokens = early_ref[:, i] if i < 4 else late_ref[:, 6 * (i - 4) : 6 * (i - 3)]
+        tokens = early_ref[:, 6 * i : 6 * i + 6] if i < 4 else late_ref[:, 6 * i - 24 : 6 * i - 18]
         normed = normalize(tokens.reshape(TOKENS, CHANNELS), gain_ref[...])
         biases.append(dot_nt(weight, normed).astype(BF16).astype(F32))
     bias = jnp.concatenate(biases, axis=0) * LOG2E
@@ -372,14 +337,14 @@
 
 def single_attend(place, early, late, gain, weight, pair, shared, rep):
     shape = (8, 7, 16, CHANNELS)
-    last = lambda *_: (0, 3 * MINE, 0, 0)
+    last = lambda *_: (0, 6 * MINE, 0, 0)
     return pl.pallas_call(
         single_kernel,
         grid_spec=pltpu.PrefetchScalarGridSpec(
             num_scalar_prefetch=1,
             grid=(1,),
             in_specs=[
-                whole((8, 4, 2, ROWS, CHANNELS)),
+                whole((8, 4 * MINE, 16, CHANNELS)),
                 whole((8, 2 * MINE + 1, 16, CHANNELS)),
                 whole((1, CHANNELS)),
                 whole((SINGLE_HEADS, CHANNELS)),
@@ -469,50 +434,35 @@
     shared = lax.dynamic_slice_in_dim(shared, 7 * x, 7, 0)
     message = jnp.concatenate(
         [
-            groups[:, 3 * MINE :],
+            groups,
             extra.reshape(8, 1, 16, CHANNELS),
             jnp.broadcast_to(shared[None], (8, 7, 16, CHANNELS)),
         ],
         axis=1,
     )
-    near, pieces = lax.optimization_barrier((groups[:, : 3 * MINE], pieces))
-    near = exchange(near)
-    message, near = lax.optimization_barrier((message, near))
-    far = exchange(message)
+    message, pieces = lax.optimization_barrier((message, pieces))
+    pair = exchange(message)
+
+    depth = 2 * lax.axis_index("zh") + lax.axis_index("zl")
+    own = join(jnp.stack([lax.axis_index("y"), depth]), pieces)
+    after = shift(own, "x", -1)
+    before = shift(own, "x", 1)
+    firsts = [own, after, shift(after[:2], "x", -1), shift(before[2:], "x", 1), before]
 
     turned = jnp.where(second_core, jnp.roll(pair_proj, 128, axis=2), pair_proj)
     wo = jnp.where(second_core, jnp.roll(pair_out_weight, 128, axis=0), pair_out_weight)
-    weights = (pair_gain, turned[0], turned[1].T, turned[2], turned[3])
-    held = project(near, *weights, 0, ())
-
-    depth = 2 * lax.axis_index("zh") + lax.axis_index("zl")
-    chunks = join(jnp.stack([lax.axis_index("y"), depth]), pieces)
-    firsts = [around(chunks[0], "x")]
-    chunk, firsts[0][1] = lax.optimization_barrier((chunks[1], firsts[0][1]))
-    firsts.append(around(chunk, "x"))
-    seconds = [[shift(item, "core", 1) for item in items] for items in firsts]
-    shared = far[:, 3 * MINE + 1 :]
-    shared, _ = lax.optimization_barrier((shared, firsts[1][1]))
+    held = project(pair, pair_gain, turned[0], turned[1].T, turned[2], turned[3])
+    seconds = [shift(item, "core", 1) for item in firsts]
+    shared = pair[:, 6 * MINE + 1 :]
+    shared, _ = lax.optimization_barrier((shared, firsts))
     shared = around(shared, "x")
     swapped = [shift(item, "core", 1) for item in shared]
 
-    held = project(far, *weights, MINE // 2, held)
-    kt, v = held[:2]
-    tokens = [list(held[2 + chunk :: 2]) for chunk in range(2)]
-    biases = [firsts[chunk] + seconds[chunk] for chunk in range(2)]
-    parts = [(tokens[chunk], biases[chunk]) for chunk in range(2)]
     x1 = x.reshape(1)
-    shape = (8, 4, 2, ROWS, CHANNELS)
-    early = attend(
-        x1, kt, v, wo, parts[:1], 4, 0, (8, 1, 2, 16, CHANNELS), lambda i, x: (0, i, 0, 2, 0), shape, None, 12
-    )
-    early = attend(
-        x1, kt, v, wo, parts[1:], 4, 0, (8, 1, 2, 32, CHANNELS), lambda i, x: (0, i, 0, 0, 0), shape, early, 22
-    )
+    biases = firsts + seconds
+    early = attend(x1, *held, pair, wo, biases, 4, 0, 4 * MINE, 30)
     early, _ = lax.optimization_barrier((early, shared))
-    late = attend(
-        x1, kt, v, wo, parts, 2, 4, (8, 6, 16, CHANNELS), lambda i, x: (0, i, 0, 0), (8, 13, 16, CHANNELS), None, 16
-    )
+    late = attend(x1, *held, pair, wo, biases, 2, 4, 2 * MINE + 1, 16)
     rep = lax.dynamic_slice_in_dim(single_rep, row * ROWS + col * MINE, MINE, 0)
     late = single_attend(
         jnp.concatenate([length, x1, core.reshape(1)]),
@@ -520,7 +470,7 @@
         late,
         bias_norm_gain.reshape(1, CHANNELS),
         single_bias_weight.T,
-        far,
+        pair,
         shared + swapped,
         rep,
     )

time: 221 us -> 198 us (0.90)
  starting transfers between devices: 42.1 us -> 28 us
  Pallas kernels: 86.1 us -> 78.5 us
  local copies, waits for them, and re-layouts: 13.4 us -> 11 us
    all_to_all x3 -> x2, starting transfers between devices: 14.9 us -> 7.23 us  [exchange(): return lax.all_to_all(value, COL, split_axis=0, concat_axis=0, tiled=True)]
    pallas_call x5 -> x3, Pallas kernels: 65.1 us -> 57.8 us  [the longest x2 49.2 us: attend(): pl.pallas_call(attend_kernel, grid_spec=pltpu.PrefetchScalarGridSpec(num_...]
    ppermute x28 -> x23, starting transfers between devices: 27.2 us -> 20.7 us  [shift(): return lax.ppermute(value, axis, pairs)]
    unnamed x55 -> x29, local copies, waits for them, and re-layouts: 5.53 us -> 2.59 us
    all_to_all x3 -> x2, waiting for transfers between devices: 2.77 us -> 0.01 us  [exchange(): return lax.all_to_all(value, COL, split_axis=0, concat_axis=0, tiled=True)]
    ppermute x28 -> x23, waiting for transfers between devices: 45.2 us -> 47.8 us  [shift(): return lax.ppermute(value, axis, pairs)]
  transfers between devices with their start and end apart: 31 -> 25, of which waited for: 10 -> 8; matrix products, arithmetic and copies ran while one was open for 5% -> 6% of each run, Pallas kernels for 36% -> 35%
where the time goes in v3:
time: 198 us; the launch traced here: 197 us
  Pallas kernels  78.5 us (40%)
  waiting for transfers between devices  47.8 us (24%)
  starting transfers between devices  28 us (14%)
  blocking collectives  22.4 us (11%)
  local copies, waits for them, and re-layouts  11 us (6%)
  other arithmetic  7.29 us (4%)
    pallas_call x2, Pallas kernels, attend(): pl.pallas_call(attend_kernel, grid_spec=pltpu.PrefetchScalarGridSpec(num_...  49.2 us
    ppermute x23, waiting for transfers between devices, shift(): return lax.ppermute(value, axis, pairs)  47.8 us
    all_to_all x1, blocking collectives, exchange(): return lax.all_to_all(value, COL, split_axis=0, concat_axis=0, tiled=True)  22.4 us
    ppermute x23, starting transfers between devices, shift(): return lax.ppermute(value, axis, pairs)  20.7 us
    pallas_call x1, Pallas kernels, project(): pl.pallas_call(project_kernel, grid=(MINE,), in_specs=[pl.BlockSpec((8, 6...  8.57 us
    pallas_call x1, Pallas kernels, single_attend(): pl.pallas_call(single_kernel, grid_spec=pltpu.PrefetchScalarGridSpec(num_...  7.24 us
    all_to_all x2, starting transfers between devices, exchange(): return lax.all_to_all(value, COL, split_axis=0, concat_axis=0, tiled=True)  7.23 us
    pallas_call x1, Pallas kernels, local_bias(): pl.pallas_call(local_bias_kernel, grid_spec=pltpu.PrefetchScalarGridSpec(...  5.76 us
  transfers between devices with their start and end apart: 25, of which 8 were waited for; matrix products, arithmetic and copies ran while one was open for 6% of the time, Pallas kernels for 35%

profile of v3, /device:TPU:0, one launch (start us, length us, event | category | flops | bytes accessed | tf_op | source)
XLA Modules:
  0.0 196.6 jit_solution(5737405269200544179)
XLA Ops:
  1.3 5.8 %shard_map.131 = bf16[2,48,384]{2,1,0:T(8,128)(2,1)} custom-call(s32[1]{0:T(128)S(6)} %sub.10.limit_ref, bf16[48,96,256]{2,1,0:T(8,128)(2,1)} %pair_ref.1, f32[1,256]{1,0:T(1,128)} %bitcast.56, bf16[8,256]{1,0:T(8,128)(2,1)} %bitcast.58), custom_call_target="tpu_custom_call" | custom-call | flops 50000000 | bytes 150000 | tf_op jit(solution)/shard_map/pallas_call | solution.py:79
  7.1 0.8 dynamic-slice_bitcast_fusion
  8.0 0.6 pad_add_fusion.place_ref
  8.6 0.6 pad_add_fusion.1.place_ref
  9.2 0.6 reshape.104.gain_ref
  9.9 3.2 %collective-permute-start.1 = (bf16[2,48,384]{2,1,0:T(8,128)(2,1)S(1)}, bf16[2,48,384]{2,1,0:T(8,128)(2,1)S(1)}, u32[]{:S(2)}, u32[]{:S(2)}) collective-permute-start(bf16[2,48,384]{2,1,0:T(8,128)(2,1)S(1)} %maximum_select_fusion.3), channel_id=1, source_target_pairs={{0,6},{2,0},{4,2},{6,4},{1,7},{3,1},{5,3},{7,5},{8,14},{10,8},{12,... | collective-permute-start | bytes 221192 | tf_op jit(solution)/shard_map/ppermute | solution.py:379
  13.1 0.6 collective-permute-start.2
  13.7 1.0 collective-permute-start.3
  14.7 2.2 %collective-permute-done.1 = bf16[2,48,384]{2,1,0:T(8,128)(2,1)S(1)} collective-permute-done((bf16[2,48,384]{2,1,0:T(8,128)(2,1)S(1)}, bf16[2,48,384]{2,1,0:T(8,128)(2,1)S(1)}, u32[]{:S(2)}, u32[]{:S(2)}) %collective-permute-start.1) | collective-permute-done | bytes 73760 | tf_op jit(solution)/shard_map/ppermute | solution.py:379
  16.8 2.8 %collective-permute-done.2 = bf16[2,48,384]{2,1,0:T(8,128)(2,1)S(1)} collective-permute-done((bf16[2,48,384]{2,1,0:T(8,128)(2,1)S(1)}, bf16[2,48,384]{2,1,0:T(8,128)(2,1)S(1)}, u32[]{:S(2)}, u32[]{:S(2)}) %collective-permute-start.2) | collective-permute-done | bytes 73760 | tf_op jit(solution)/shard_map/ppermute | solution.py:379
  19.7 0.8 collective-permute-done.3
  20.6 4.1 %collective-permute-start.4 = (bf16[4,2,48,384]{3,2,1,0:T(8,128)(2,1)S(1)}, bf16[4,2,48,384]{3,2,1,0:T(8,128)(2,1)S(1)}, u32[]{:S(2)}, u32[]{:S(2)}) collective-permute-start(bf16[4,2,48,384]{3,2,1,0:T(8,128)(2,1)S(1)} %pad_maximum_fusion.2.a_ref), channel_id=1, source_target_pairs={{0,17},{16,0},{1,16},{17,1},{2,19},{18,2},{3,18},{19,3},{4,21},{20... | collective-permute-start | bytes 884744 | tf_op jit(solution)/shard_map/ppermute | solution.py:379
  24.7 1.3 collective-permute-start.6
  26.0 4.1 %shard_map.132 = (bf16[2,2,48,768]{3,2,1,0:T(8,128)(2,1)}, f32[2,48,96]{2,1,0:T(8,128)}) custom-call(s32[2]{0:T(128)} %pad_add_fusion.place_ref, bf16[768,768]{1,0:T(8,128)(2,1)} %single_ref, f32[1,768]{1,0:T(1,128)} %reshape.104.gain_ref, bf16[4,96,768]{2,1,0:T(8,128)(2,1)} %bitcast.48), custom_call_target="tpu_custom_call" | custom-call | flops 40000000 | bytes 120000 | tf_op jit(solution)/shard_map/pallas_call | solution.py:251
  30.1 0.9 constant_dynamic-slice_fusion.2
  31.3 0.8 convert_element_type.7
  32.3 1.9 pad_maximum_fusion
  34.2 3.3 %collective-permute-done.4.b_ref = bf16[4,2,48,384]{3,2,1,0:T(8,128)(2,1)S(1)} collective-permute-done((bf16[4,2,48,384]{3,2,1,0:T(8,128)(2,1)S(1)}, bf16[4,2,48,384]{3,2,1,0:T(8,128)(2,1)S(1)}, u32[]{:S(2)}, u32[]{:S(2)}) %collective-permute-start.4) | collective-permute-done | bytes 294944 | tf_op jit(solution)/shard_map/ppermute | solution.py:379
  37.4 3.5 %collective-permute-done.6.d_ref = bf16[4,2,48,384]{3,2,1,0:T(8,128)(2,1)} collective-permute-done((bf16[4,2,48,384]{3,2,1,0:T(8,128)(2,1)S(1)}, bf16[4,2,48,384]{3,2,1,0:T(8,128)(2,1)}, u32[]{:S(2)}, u32[]{:S(2)}) %collective-permute-start.6) | collective-permute-done | bytes 294944 | tf_op jit(solution)/shard_map/ppermute | solution.py:379
  40.9 3.6 %shard_map.134.rest_0_ = bf16[4,192,768]{2,1,0:T(8,128)(2,1)} custom-call(s32[2]{0:T(128)} %pad_add_fusion.1.place_ref, bf16[4,2,48,384]{3,2,1,0:T(8,128)(2,1)} %copy-done.4, bf16[4,2,48,384]{3,2,1,0:T(8,128)(2,1)} %copy-done.7, bf16[4,2,48,384]{3,2,1,0:T(8,128)(2,1)} %collective-permute-done.5.c_ref, bf16[4,2,48,384]{3,2,1,0:T(8,128)(2,1)} %collective-permute-done.6.d_ref), custom_call_target="tpu_custom_call" | custom-call | flops 30000000 | bytes 90000 | tf_op jit(solution)/shard_map/pallas_call | solution.py:119
  44.6 2.8 %collective-permute-start.7 = (bf16[4,192,768]{2,1,0:T(8,128)(2,1)}, bf16[4,192,768]{2,1,0:T(8,128)(2,1)}, u32[]{:S(2)}, u32[]{:S(2)}) collective-permute-start(bf16[4,192,768]{2,1,0:T(8,128)(2,1)} %shard_map.134.rest_0_), channel_id=1, source_target_pairs={{0,96},{32,0},{64,32},{96,64},{1,97},{33,1},{65,33},{97,65},{2,98}... | collective-permute-start | bytes 3538952 | tf_op jit(solution)/shard_map/ppermute | solution.py:379
  47.3 3.6 %all-to-all-start = ((bf16[8,44,16,256]{3,2,1,0:T(8,128)(2,1)}), bf16[8,44,16,256]{3,2,1,0:T(8,128)(2,1)S(1)}, u32[]{:S(2)}, u32[]{:S(2)}) async-start(bf16[8,44,16,256]{3,2,1,0:T(8,128)(2,1)} %pad_maximum_fusion), calls=%async_computation | async-start | bytes 5767168 | tf_op jit(solution)/shard_map/all_to_all | solution.py:366
  51.0 21.7 %collective-permute-done.7.rest_1_ = bf16[4,192,768]{2,1,0:T(8,128)(2,1)} collective-permute-done((bf16[4,192,768]{2,1,0:T(8,128)(2,1)}, bf16[4,192,768]{2,1,0:T(8,128)(2,1)}, u32[]{:S(2)}, u32[]{:S(2)}) %collective-permute-start.7) | collective-permute-done | bytes 1179680 | tf_op jit(solution)/shard_map/ppermute | solution.py:379
  72.7 1.1 slice.60
  73.8 3.8 %collective-permute-start.8 = (bf16[2,192,768]{2,1,0:T(8,128)(2,1)S(1)}, bf16[2,192,768]{2,1,0:T(8,128)(2,1)}, u32[]{:S(2)}, u32[]{:S(2)}) collective-permute-start(bf16[2,192,768]{2,1,0:T(8,128)(2,1)S(1)} %slice.60), channel_id=1, source_target_pairs={{0,96},{32,0},{64,32},{96,64},{1,97},{33,1},{65,33},{97,65},{2,98}... | collective-permute-start | bytes 1769480 | tf_op jit(solution)/shard_map/ppermute | solution.py:379
  77.6 1.1 slice.61
  79.0 0.5 collective-permute-start.12
  79.7 0.8 slice_bitcast_fusion
  80.5 8.7 %collective-permute-done.8.rest_2_ = bf16[2,192,768]{2,1,0:T(8,128)(2,1)} collective-permute-done((bf16[2,192,768]{2,1,0:T(8,128)(2,1)S(1)}, bf16[2,192,768]{2,1,0:T(8,128)(2,1)}, u32[]{:S(2)}, u32[]{:S(2)}) %collective-permute-start.8) | collective-permute-done | bytes 589856 | tf_op jit(solution)/shard_map/ppermute | solution.py:379
  89.1 4.7 %collective-permute-done.10.rest_3_ = bf16[2,192,768]{2,1,0:T(8,128)(2,1)} collective-permute-done((bf16[2,192,768]{2,1,0:T(8,128)(2,1)S(1)}, bf16[2,192,768]{2,1,0:T(8,128)(2,1)}, u32[]{:S(2)}, u32[]{:S(2)}) %collective-permute-start.10) | collective-permute-done | bytes 589856 | tf_op jit(solution)/shard_map/ppermute | solution.py:379
  93.8 0.7 pad_add_fusion.2.place_ref
  94.5 0.8 copy.23.wkt_ref
  95.3 1.3 constant_dynamic-slice_fusion.rest_8_
  96.6 0.7 maximum_select_fusion.1.wo_ref
  97.4 1.5 copy-done.1
  98.9 8.6 %shard_map.133 = (bf16[6,256,768]{2,1,0:T(8,128)(2,1)}, bf16[6,768,256]{2,1,0:T(8,128)(2,1)}, bf16[6,4,192,256]{3,2,1,0:T(8,128)(2,1)}, bf16[6,4,192,256]{3,2,1,0:T(8,128)(2,1)}) custom-call(bf16[8,44,16,256]{3,2,1,0:T(8,128)(2,1)} %copy-done.1, f32[1,256]{1,0:T(1,128)} %bitcast.57, bf16[256,256]{1,0:T(8,128)(2,1)} %get-tuple-element.39.wq_ref, ...), custom_call_target="tpu_custom_call" | custom-call | flops 50000000 | bytes 150000 | tf_op jit(solution)/shard_map/pallas_call | solution.py:152
  107.5 1.1 collective-permute-start.17
  108.7 1.0 collective-permute-start.18
  109.6 31.1 %shard_map.135.early_ref = bf16[8,24,16,256]{3,2,1,0:T(8,128)(2,1)} custom-call(s32[1]{0:T(128)} %bitcast.x_ref, bf16[6,256,768]{2,1,0:T(8,128)(2,1)} %get-tuple-element.24.kt_ref, bf16[6,768,256]{2,1,0:T(8,128)(2,1)} %get-tuple-element.25.v_ref, bf16[6,4,192,256]{3,2,1,0:T(8,128)(2,1)} %get-tuple-element.26.q_ref, ...), custom_call_target="tpu_custom_call" | custom-call | flops 30000001024 | bytes 90000000 | tf_op jit(solution)/shard_map/pallas_call | solution.py:213
  140.8 3.6 %all-to-all-start.1 = ((bf16[8,24,16,256]{3,2,1,0:T(8,128)(2,1)}), bf16[8,24,16,256]{3,2,1,0:T(8,128)(2,1)S(1)}, u32[]{:S(2)}, u32[]{:S(2)}) async-start(bf16[8,24,16,256]{3,2,1,0:T(8,128)(2,1)} %shard_map.135.early_ref), calls=%async_computation.1 | async-start | bytes 3145728 | tf_op jit(solution)/shard_map/all_to_all | solution.py:366
  144.4 0.6 collective-permute-start.20
  145.1 0.4 collective-permute-start.22
  145.5 18.1 %shard_map.136.late_ref = bf16[8,13,16,256]{3,2,1,0:T(8,128)(2,1)} custom-call(s32[1]{0:T(128)} %bitcast.x_ref, bf16[6,256,768]{2,1,0:T(8,128)(2,1)} %get-tuple-element.24.kt_ref, bf16[6,768,256]{2,1,0:T(8,128)(2,1)} %get-tuple-element.25.v_ref, bf16[6,4,192,256]{3,2,1,0:T(8,128)(2,1)} %get-tuple-element.26.q_ref, ...), custom_call_target="tpu_custom_call" | custom-call | flops 16000000000 | bytes 48000000 | tf_op jit(solution)/shard_map/pallas_call | solution.py:213
  163.7 0.7 copy-done.11
  164.7 7.2 %shard_map.137 = bf16[8,13,16,256]{3,2,1,0:T(8,128)(2,1)} custom-call(s32[3]{0:T(128)} %pad_add_fusion.2.place_ref, bf16[8,24,16,256]{3,2,1,0:T(8,128)(2,1)} %shard_map.135.early_ref, bf16[8,13,16,256]{3,2,1,0:T(8,128)(2,1)} %shard_map.136.late_ref, f32[1,256]{1,0:T(1,128)} %bitcast.60, bf16[16,256]{1,0:T(8,128)(2,1)} %bitcast.59, ...), custom_call_target="tpu_custom_call", output_to_operand_aliasing={{}: (2, {})} | custom-call | flops 7000000000 | bytes 21000000 | tf_op jit(solution)/shard_map/pallas_call | solution.py:341
  171.9 22.4 %all_to_all.15 = bf16[8,13,16,256]{3,2,1,0:T(8,128)(2,1)S(1)} all-to-all(bf16[8,13,16,256]{3,2,1,0:T(8,128)(2,1)} %shard_map.137), channel_id=1, replica_groups=mesh['x'=4,'zl'=2,'core'=2,'y'=4,'zh'=2] {'y','zh'}, dimensions={0} | all-to-all | bytes 1703936 | tf_op jit(solution)/shard_map/all_to_all | solution.py:366
  194.3 0.6 reshape_squeeze.3
  195.0 1.6 pad_maximum_fusion.1
  (73 shorter events, 1.8 us)
Async XLA Ops:
  0.6 8.0 %copy-start = (bf16[96,768]{1,0:T(8,128)(2,1)S(1)}, bf16[96,768]{1,0:T(8,128)(2,1)}, u32[]{:S(2)}) copy-start(bf16[96,768]{1,0:T(8,128)(2,1)} %param.23) | copy-start | bytes 442372
  0.6 8.6 %copy-start.8 = (f32[768]{0:T(1024)S(1)}, f32[768]{0:T(1024)}, u32[]{:S(2)}) copy-start(f32[768]{0:T(1024)} %param.19) | copy-start | bytes 9220
  7.9 2.0 collective-permute-start
  9.9 7.0 %collective-permute-start.1 = (bf16[2,48,384]{2,1,0:T(8,128)(2,1)S(1)}, bf16[2,48,384]{2,1,0:T(8,128)(2,1)S(1)}, u32[]{:S(2)}, u32[]{:S(2)}) collective-permute-start(bf16[2,48,384]{2,1,0:T(8,128)(2,1)S(1)} %maximum_select_fusion.3), channel_id=1, source_target_pairs={{0,6},{2,0},{4,2},{6,4},{1,7},{3,1},{5,3},{7,5},{8,14},{10,8},{12,... | collective-permute-start | bytes 221192 | tf_op jit(solution)/shard_map/ppermute | solution.py:379
  13.1 6.6 %collective-permute-start.2 = (bf16[2,48,384]{2,1,0:T(8,128)(2,1)S(1)}, bf16[2,48,384]{2,1,0:T(8,128)(2,1)S(1)}, u32[]{:S(2)}, u32[]{:S(2)}) collective-permute-start(bf16[2,48,384]{2,1,0:T(8,128)(2,1)S(1)} %maximum_select_fusion.3), channel_id=1, source_target_pairs={{0,4},{2,6},{4,0},{6,2},{1,5},{3,7},{5,1},{7,3},{8,12},{10,14},{12... | collective-permute-start | bytes 221192 | tf_op jit(solution)/shard_map/ppermute | solution.py:379
  13.7 6.8 %collective-permute-start.3 = (bf16[2,48,384]{2,1,0:T(8,128)(2,1)S(1)}, bf16[2,48,384]{2,1,0:T(8,128)(2,1)S(1)}, u32[]{:S(2)}, u32[]{:S(2)}) collective-permute-start(bf16[2,48,384]{2,1,0:T(8,128)(2,1)S(1)} %maximum_select_fusion.3), channel_id=1, source_target_pairs={{0,2},{2,4},{4,6},{6,0},{1,3},{3,5},{5,7},{7,1},{8,10},{10,12},{12... | collective-permute-start | bytes 221192 | tf_op jit(solution)/shard_map/ppermute | solution.py:379
  20.6 13.6 %copy-start.4 = (bf16[4,2,48,384]{3,2,1,0:T(8,128)(2,1)}, bf16[4,2,48,384]{3,2,1,0:T(8,128)(2,1)S(1)}, u32[]{:S(2)}) copy-start(bf16[4,2,48,384]{3,2,1,0:T(8,128)(2,1)S(1)} %pad_maximum_fusion.2.a_ref) | copy-start | bytes 884740
  20.6 11.7 %copy-start.2 = (bf16[48,96,256]{2,1,0:T(8,128)(2,1)S(1)}, bf16[48,96,256]{2,1,0:T(8,128)(2,1)}, u32[]{:S(2)}) copy-start(bf16[48,96,256]{2,1,0:T(8,128)(2,1)} %pair_ref.1) | copy-start | bytes 7077892
  20.6 16.8 %collective-permute-start.4 = (bf16[4,2,48,384]{3,2,1,0:T(8,128)(2,1)S(1)}, bf16[4,2,48,384]{3,2,1,0:T(8,128)(2,1)S(1)}, u32[]{:S(2)}, u32[]{:S(2)}) collective-permute-start(bf16[4,2,48,384]{3,2,1,0:T(8,128)(2,1)S(1)} %pad_maximum_fusion.2.a_ref), channel_id=1, source_target_pairs={{0,17},{16,0},{1,16},{17,1},{2,19},{18,2},{3,18},{19,3},{4,21},{20... | collective-permute-start | bytes 884744 | tf_op jit(solution)/shard_map/ppermute | solution.py:379
  24.7 12.7 %collective-permute-start.5 = (bf16[4,2,48,384]{3,2,1,0:T(8,128)(2,1)S(1)}, bf16[4,2,48,384]{3,2,1,0:T(8,128)(2,1)}, u32[]{:S(2)}, u32[]{:S(2)}) collective-permute-start(bf16[4,2,48,384]{3,2,1,0:T(8,128)(2,1)S(1)} %pad_maximum_fusion.2.a_ref), channel_id=1, source_target_pairs={{0,1},{16,17},{1,0},{17,16},{2,3},{18,19},{3,2},{19,18},{4,5},{20,... | collective-permute-start | bytes 884744 | tf_op jit(solution)/shard_map/ppermute | solution.py:379
  24.7 16.3 %collective-permute-start.6 = (bf16[4,2,48,384]{3,2,1,0:T(8,128)(2,1)S(1)}, bf16[4,2,48,384]{3,2,1,0:T(8,128)(2,1)}, u32[]{:S(2)}, u32[]{:S(2)}) collective-permute-start(bf16[4,2,48,384]{3,2,1,0:T(8,128)(2,1)S(1)} %pad_maximum_fusion.2.a_ref), channel_id=1, source_target_pairs={{0,16},{16,1},{1,17},{17,0},{2,18},{18,3},{3,19},{19,2},{4,20},{20... | collective-permute-start | bytes 884744 | tf_op jit(solution)/shard_map/ppermute | solution.py:379
  37.4 3.5 %copy-start.7 = (bf16[4,2,48,384]{3,2,1,0:T(8,128)(2,1)}, bf16[4,2,48,384]{3,2,1,0:T(8,128)(2,1)S(1)}, u32[]{:S(2)}) copy-start(bf16[4,2,48,384]{3,2,1,0:T(8,128)(2,1)S(1)} %collective-permute-done.4.b_ref) | copy-start | bytes 884740
  44.6 28.2 %collective-permute-start.7 = (bf16[4,192,768]{2,1,0:T(8,128)(2,1)}, bf16[4,192,768]{2,1,0:T(8,128)(2,1)}, u32[]{:S(2)}, u32[]{:S(2)}) collective-permute-start(bf16[4,192,768]{2,1,0:T(8,128)(2,1)} %shard_map.134.rest_0_), channel_id=1, source_target_pairs={{0,96},{32,0},{64,32},{96,64},{1,97},{33,1},{65,33},{97,65},{2,98}... | collective-permute-start | bytes 3538952 | tf_op jit(solution)/shard_map/ppermute | solution.py:379
  47.3 30.3 %collective-permute-start.9 = (bf16[4,192,768]{2,1,0:T(8,128)(2,1)}, bf16[4,192,768]{2,1,0:T(8,128)(2,1)}, u32[]{:S(2)}, u32[]{:S(2)}) collective-permute-start(bf16[4,192,768]{2,1,0:T(8,128)(2,1)} %shard_map.134.rest_0_), channel_id=1, source_target_pairs={{0,32},{32,64},{64,96},{96,0},{1,33},{33,65},{65,97},{97,1},{2,34}... | collective-permute-start | bytes 3538952 | tf_op jit(solution)/shard_map/ppermute | solution.py:379
  47.3 50.0 %all-to-all-start = ((bf16[8,44,16,256]{3,2,1,0:T(8,128)(2,1)}), bf16[8,44,16,256]{3,2,1,0:T(8,128)(2,1)S(1)}, u32[]{:S(2)}, u32[]{:S(2)}) async-start(bf16[8,44,16,256]{3,2,1,0:T(8,128)(2,1)} %pad_maximum_fusion), calls=%async_computation | async-start | bytes 5767168 | tf_op jit(solution)/shard_map/all_to_all | solution.py:366
  51.0 27.8 %copy-start.3 = (bf16[4,256,256]{2,1,0:T(8,128)(2,1)S(1)}, bf16[4,256,256]{2,1,0:T(8,128)(2,1)}, u32[]{:S(2)}) copy-start(bf16[4,256,256]{2,1,0:T(8,128)(2,1)} %param.16) | copy-start | bytes 1572868
  73.8 22.8 %copy-start.5 = (bf16[256,256]{1,0:T(8,128)(2,1)S(1)}, bf16[256,256]{1,0:T(8,128)(2,1)}, u32[]{:S(2)}) copy-start(bf16[256,256]{1,0:T(8,128)(2,1)} %param.18) | copy-start | bytes 393220
  73.8 15.3 %collective-permute-start.8 = (bf16[2,192,768]{2,1,0:T(8,128)(2,1)S(1)}, bf16[2,192,768]{2,1,0:T(8,128)(2,1)}, u32[]{:S(2)}, u32[]{:S(2)}) collective-permute-start(bf16[2,192,768]{2,1,0:T(8,128)(2,1)S(1)} %slice.60), channel_id=1, source_target_pairs={{0,96},{32,0},{64,32},{96,64},{1,97},{33,1},{65,33},{97,65},{2,98}... | collective-permute-start | bytes 1769480 | tf_op jit(solution)/shard_map/ppermute | solution.py:379
  78.7 15.1 %collective-permute-start.10 = (bf16[2,192,768]{2,1,0:T(8,128)(2,1)S(1)}, bf16[2,192,768]{2,1,0:T(8,128)(2,1)}, u32[]{:S(2)}, u32[]{:S(2)}) collective-permute-start(bf16[2,192,768]{2,1,0:T(8,128)(2,1)S(1)} %slice.61), channel_id=1, source_target_pairs={{0,32},{32,64},{64,96},{96,0},{1,33},{33,65},{65,97},{97,1},{2,34}... | collective-permute-start | bytes 1769480 | tf_op jit(solution)/shard_map/ppermute | solution.py:379
  78.9 28.5 %collective-permute-start.11 = (bf16[4,192,768]{2,1,0:T(8,128)(2,1)}, bf16[4,192,768]{2,1,0:T(8,128)(2,1)}, u32[]{:S(2)}, u32[]{:S(2)}) collective-permute-start(bf16[4,192,768]{2,1,0:T(8,128)(2,1)} %shard_map.134.rest_0_), channel_id=1, source_target_pairs={{0,8},{8,0},{1,9},{9,1},{2,10},{10,2},{3,11},{11,3},{4,12},{12,4},... | collective-permute-start | bytes 3538952 | tf_op jit(solution)/shard_map/ppermute | solution.py:379
  79.0 30.6 %collective-permute-start.12 = (bf16[4,192,768]{2,1,0:T(8,128)(2,1)}, bf16[4,192,768]{2,1,0:T(8,128)(2,1)}, u32[]{:S(2)}, u32[]{:S(2)}) collective-permute-start(bf16[4,192,768]{2,1,0:T(8,128)(2,1)} %collective-permute-done.7.rest_1_), channel_id=1, source_target_pairs={{0,8},{8,0},{1,9},{9,1},{2,10},{10,2},{3,11},{11,3},{4,12},{12,4},... | collective-permute-start | bytes 3538952 | tf_op jit(solution)/shard_map/ppermute | solution.py:379
  79.5 30.1 %collective-permute-start.15 = (bf16[4,192,768]{2,1,0:T(8,128)(2,1)}, bf16[4,192,768]{2,1,0:T(8,128)(2,1)}, u32[]{:S(2)}, u32[]{:S(2)}) collective-permute-start(bf16[4,192,768]{2,1,0:T(8,128)(2,1)} %collective-permute-done.9.rest_4_), channel_id=1, source_target_pairs={{0,8},{8,0},{1,9},{9,1},{2,10},{10,2},{3,11},{11,3},{4,12},{12,4},... | collective-permute-start | bytes 3538952 | tf_op jit(solution)/shard_map/ppermute | solution.py:379
  89.1 18.4 %collective-permute-start.13 = (bf16[2,192,768]{2,1,0:T(8,128)(2,1)}, bf16[2,192,768]{2,1,0:T(8,128)(2,1)}, u32[]{:S(2)}, u32[]{:S(2)}) collective-permute-start(bf16[2,192,768]{2,1,0:T(8,128)(2,1)} %collective-permute-done.8.rest_2_), channel_id=1, source_target_pairs={{0,8},{8,0},{1,9},{9,1},{2,10},{10,2},{3,11},{11,3},{4,12},{12,4},... | collective-permute-start | bytes 1769480 | tf_op jit(solution)/shard_map/ppermute | solution.py:379
  93.8 14.8 %collective-permute-start.14 = (bf16[2,192,768]{2,1,0:T(8,128)(2,1)}, bf16[2,192,768]{2,1,0:T(8,128)(2,1)}, u32[]{:S(2)}, u32[]{:S(2)}) collective-permute-start(bf16[2,192,768]{2,1,0:T(8,128)(2,1)} %collective-permute-done.10.rest_3_), channel_id=1, source_target_pairs={{0,8},{8,0},{1,9},{9,1},{2,10},{10,2},{3,11},{11,3},{4,12},{12,4},... | collective-permute-start | bytes 1769480 | tf_op jit(solution)/shard_map/ppermute | solution.py:379
  97.3 1.5 copy-start.1
  97.4 43.4 %copy-start.6 = (bf16[8,7,16,256]{3,2,1,0:T(8,128)(2,1)}, bf16[8,7,16,256]{3,2,1,0:T(8,128)(2,1)S(1)}, u32[]{:S(2)}) copy-start(bf16[8,7,16,256]{3,2,1,0:T(8,128)(2,1)S(1)} %slice.62.rest_0_) | copy-start | bytes 1376260
  107.4 33.3 %collective-permute-start.16 = (bf16[8,7,16,256]{3,2,1,0:T(8,128)(2,1)S(1)}, bf16[8,7,16,256]{3,2,1,0:T(8,128)(2,1)S(1)}, u32[]{:S(2)}, u32[]{:S(2)}) collective-permute-start(bf16[8,7,16,256]{3,2,1,0:T(8,128)(2,1)S(1)} %slice.62.rest_0_), channel_id=1, source_target_pairs={{0,96},{32,0},{64,32},{96,64},{1,97},{33,1},{65,33},{97,65},{2,98}... | collective-permute-start | bytes 1376264 | tf_op jit(solution)/shard_map/ppermute | solution.py:379
  107.5 33.3 %collective-permute-start.17 = (bf16[8,7,16,256]{3,2,1,0:T(8,128)(2,1)S(1)}, bf16[8,7,16,256]{3,2,1,0:T(8,128)(2,1)S(1)}, u32[]{:S(2)}, u32[]{:S(2)}) collective-permute-start(bf16[8,7,16,256]{3,2,1,0:T(8,128)(2,1)S(1)} %slice.62.rest_0_), channel_id=1, source_target_pairs={{0,64},{32,96},{64,0},{96,32},{1,65},{33,97},{65,1},{97,33},{2,66}... | collective-permute-start | bytes 1376264 | tf_op jit(solution)/shard_map/ppermute | solution.py:379
  108.7 32.2 %collective-permute-start.18 = (bf16[8,7,16,256]{3,2,1,0:T(8,128)(2,1)S(1)}, bf16[8,7,16,256]{3,2,1,0:T(8,128)(2,1)}, u32[]{:S(2)}, u32[]{:S(2)}) collective-permute-start(bf16[8,7,16,256]{3,2,1,0:T(8,128)(2,1)S(1)} %slice.62.rest_0_), channel_id=1, source_target_pairs={{0,32},{32,64},{64,96},{96,0},{1,33},{33,65},{65,97},{97,1},{2,34}... | collective-permute-start | bytes 1376264 | tf_op jit(solution)/shard_map/ppermute | solution.py:379
  109.6 54.0 %collective-permute-start.19 = (bf16[8,7,16,256]{3,2,1,0:T(8,128)(2,1)S(1)}, bf16[8,7,16,256]{3,2,1,0:T(8,128)(2,1)}, u32[]{:S(2)}, u32[]{:S(2)}) collective-permute-start(bf16[8,7,16,256]{3,2,1,0:T(8,128)(2,1)S(1)} %slice.62.rest_0_), channel_id=1, source_target_pairs={{0,8},{8,0},{1,9},{9,1},{2,10},{10,2},{3,11},{11,3},{4,12},{12,4},... | collective-permute-start | bytes 1376264 | tf_op jit(solution)/shard_map/ppermute | solution.py:379
  140.8 22.8 %copy-start.9 = (bf16[8,7,16,256]{3,2,1,0:T(8,128)(2,1)}, bf16[8,7,16,256]{3,2,1,0:T(8,128)(2,1)S(1)}, u32[]{:S(2)}) copy-start(bf16[8,7,16,256]{3,2,1,0:T(8,128)(2,1)S(1)} %collective-permute-done.16.rest_1_) | copy-start | bytes 1376260
  140.8 22.8 %copy-start.10 = (bf16[8,7,16,256]{3,2,1,0:T(8,128)(2,1)}, bf16[8,7,16,256]{3,2,1,0:T(8,128)(2,1)S(1)}, u32[]{:S(2)}) copy-start(bf16[8,7,16,256]{3,2,1,0:T(8,128)(2,1)S(1)} %collective-permute-done.17.rest_2_) | copy-start | bytes 1376260
  140.8 31.1 %all-to-all-start.1 = ((bf16[8,24,16,256]{3,2,1,0:T(8,128)(2,1)}), bf16[8,24,16,256]{3,2,1,0:T(8,128)(2,1)S(1)}, u32[]{:S(2)}, u32[]{:S(2)}) async-start(bf16[8,24,16,256]{3,2,1,0:T(8,128)(2,1)} %shard_map.135.early_ref), calls=%async_computation.1 | async-start | bytes 3145728 | tf_op jit(solution)/shard_map/all_to_all | solution.py:366
  144.4 19.2 %collective-permute-start.20 = (bf16[8,7,16,256]{3,2,1,0:T(8,128)(2,1)S(1)}, bf16[8,7,16,256]{3,2,1,0:T(8,128)(2,1)S(1)}, u32[]{:S(2)}, u32[]{:S(2)}) collective-permute-start(bf16[8,7,16,256]{3,2,1,0:T(8,128)(2,1)S(1)} %collective-permute-done.16.rest_1_), channel_id=1, source_target_pairs={{0,8},{8,0},{1,9},{9,1},{2,10},{10,2},{3,11},{11,3},{4,12},{12,4},... | collective-permute-start | bytes 1376264 | tf_op jit(solution)/shard_map/ppermute | solution.py:379
  145.0 18.6 %collective-permute-start.21 = (bf16[8,7,16,256]{3,2,1,0:T(8,128)(2,1)S(1)}, bf16[8,7,16,256]{3,2,1,0:T(8,128)(2,1)S(1)}, u32[]{:S(2)}, u32[]{:S(2)}) collective-permute-start(bf16[8,7,16,256]{3,2,1,0:T(8,128)(2,1)S(1)} %collective-permute-done.17.rest_2_), channel_id=1, source_target_pairs={{0,8},{8,0},{1,9},{9,1},{2,10},{10,2},{3,11},{11,3},{4,12},{12,4},... | collective-permute-start | bytes 1376264 | tf_op jit(solution)/shard_map/ppermute | solution.py:379
  145.1 18.6 %collective-permute-start.22 = (bf16[8,7,16,256]{3,2,1,0:T(8,128)(2,1)}, bf16[8,7,16,256]{3,2,1,0:T(8,128)(2,1)S(1)}, u32[]{:S(2)}, u32[]{:S(2)}) collective-permute-start(bf16[8,7,16,256]{3,2,1,0:T(8,128)(2,1)} %collective-permute-done.18.rest_3_), channel_id=1, source_target_pairs={{0,8},{8,0},{1,9},{9,1},{2,10},{10,2},{3,11},{11,3},{4,12},{12,4},... | collective-permute-start | bytes 1376264 | tf_op jit(solution)/shard_map/ppermute | solution.py:379
  163.6 0.8 copy-start.11
  163.7 0.9 copy-start.12
  163.7 1.0 copy-start.13
